TPU v7x, 32 devices: a whole 2x2x4 slice. The times are simulated.
32 devices in a mesh: seq: 8 (over z, x), tp: 2 (over core), pd: 2 (over y).
Axes of the slice: x: 2, y: 2, z: 4, core: 2. Of those that a mesh axis runs over, the one named last changes fastest.
Arguments:
- hidden_in: bfloat16 [2, 2048, 2048], P('pd', 'seq'), may hold values from -6 to 6
- input_gain: float32 [2048], replicated, may hold values from 0.5 to 1.5
- w_query: bfloat16 [2048, 2048], P(None, 'tp'), may hold values from -0.125 to 0.125
- w_key: bfloat16 [2048, 256], P(None, 'tp'), may hold values from -0.125 to 0.125
- w_value: bfloat16 [2048, 256], P(None, 'tp'), may hold values from -0.125 to 0.125
- q_gain: float32 [128], replicated, may hold values from 0.1 to 1.9
- k_gain: float32 [128], replicated, may hold values from 0.1 to 1.9
- w_out: bfloat16 [2048, 2048], P('tp'), may hold values from -0.125 to 0.125
- post_gain: float32 [2048], replicated, may hold values from 0.5 to 1.5
- ctx_key: bfloat16 [2, 512, 256], P('pd', 'seq', 'tp'), may hold values from -70 to 70
- ctx_value: bfloat16 [2, 512, 256], P('pd', 'seq', 'tp'), may hold values from -6 to 6
- span_lens: int32 [2, 8], P('pd'), may hold values from 1 to 1024, 2048 in all within a row
- ctx_lens: int32 [2, 8], P('pd'), may hold values from 1 to 256, 512 in all within a row
- route_ids: int32 [2, 2048, 8], P('pd', ('seq', 'tp')), may hold values from 0 to 31, all different within a row; in each aligned block of 128 rows (0 to 127, 128 to 255, ..., all dimensions but the last counted through in order) at most 48 rows name the same one
- route_weights: float32 [2, 2048, 8], P('pd', ('seq', 'tp')), may hold values from 0.05 to 1
- w_gate_up: bfloat16 [32, 2048, 1536], P(('seq', 'tp', 'pd')), may hold values from -0.125 to 0.125
- w_down: bfloat16 [32, 768, 2048], P(('seq', 'tp', 'pd')), may hold values from -0.21875 to 0.21875
- earlier_kv: bfloat16 [8, 2, 2048, 2, 256], P(None, 'pd', 'seq', 'tp'), may hold values from -6 to 6
- page_table: int32 [8, 2, 16, 2], P(None, 'pd', 'seq', 'tp'), may hold values from 0 to 127, as said below
Outputs:
- layer_out: bfloat16 [2, 2048, 2048], P('pd', ('seq', 'tp'))
- decode_cache: bfloat16 [8, 2, 2, 16, 128, 256], P('seq', 'tp', 'pd')
Inputs may be any that keep to these rules, and one draw needn't show every extreme that they name: `route_ids`: within the rows of one device no expert is named more than 48 times, a bound that some block reaches. `page_table`: an entry owner * 16 + slot sends the page to that slot of the device at index owner of seq, with the same indices of tp and pd. Every slot of every owner receives exactly one page; one device sends at most 2 pages to one owner, and exactly that many to some owner.
All inputs are finite; a program needn't handle non-finite values.
Results may differ from a plain program's by a relative error of at most 0.015.
Values may be sent and summed in bfloat16 or wider, within the bound.
A program may use at most 128 MiB of HBM per device.

v0:
```python
import math

import jax
import jax.numpy as jnp
from jax import lax
from jax.sharding import PartitionSpec as P

PAGE = 128


def rms_norm(values, gain):
    return values * lax.rsqrt(jnp.mean(values * values, axis=-1, keepdims=True) + 1e-06) * gain


def rotate(values, places):
    half = values.shape[-1] // 2
    freq = jnp.exp(
        jnp.arange(half, dtype=jnp.float32) * (-2.0 * math.log(1000000.0) / values.shape[-1])
    )
    angle = places.astype(jnp.float32)[:, None] * freq[None, :]
    cosine = jnp.cos(angle)[:, None, :]
    sine = jnp.sin(angle)[:, None, :]
    first = values[..., :half]
    second = values[..., half:]
    return jnp.concatenate(
        [first * cosine - second * sine, second * cosine + first * sine], axis=-1
    )


def query_places(lengths, context_lengths, places):
    ends = jnp.cumsum(lengths)
    starts = ends - lengths
    request = jnp.sum((places[:, None] >= ends[None, :]).astype(jnp.int32), axis=1)
    member = request[:, None] == jnp.arange(lengths.shape[0], dtype=jnp.int32)[None, :]
    first = jnp.sum(jnp.where(member, starts[None, :], 0), axis=1)
    prior = jnp.sum(jnp.where(member, context_lengths[None, :], 0), axis=1)
    return (request, places - first + prior)


def context_places(context_lengths, places):
    ends = jnp.cumsum(context_lengths)
    starts = ends - context_lengths
    request = jnp.sum((places[:, None] >= ends[None, :]).astype(jnp.int32), axis=1)
    member = request[:, None] == jnp.arange(context_lengths.shape[0], dtype=jnp.int32)[None, :]
    first = jnp.sum(jnp.where(member, starts[None, :], 0), axis=1)
    return (request, places - first)


def expert_mlp(arrived, w_gate_up, w_down):
    hidden = jnp.einsum("sejd,edf->sejf", arrived, w_gate_up, preferred_element_type=jnp.float32)
    inner = hidden.shape[-1] // 2
    act = (jax.nn.silu(hidden[..., :inner]) * hidden[..., inner:]).astype(jnp.bfloat16)
    return jnp.einsum("sejf,efd->sejd", act, w_down, preferred_element_type=jnp.float32).astype(
        jnp.bfloat16
    )


def shards(
    hidden_in,
    input_gain,
    w_query,
    w_key,
    w_value,
    q_gain,
    k_gain,
    w_out,
    post_gain,
    ctx_key,
    ctx_value,
    span_lens,
    ctx_lens,
    route_ids,
    route_weights,
    w_gate_up,
    w_down,
    earlier_kv,
    page_table,
):
    tokens = hidden_in[0]
    tok_count = tokens.shape[0]
    width = tokens.shape[1]
    ctx_count = ctx_key.shape[1]
    head_dim = q_gain.shape[0]
    seq_index = lax.axis_index("seq")
    span_places = seq_index * tok_count + jnp.arange(tok_count, dtype=jnp.int32)
    ctx_index = seq_index * ctx_count + jnp.arange(ctx_count, dtype=jnp.int32)
    query_req, query_pos = query_places(span_lens[0], ctx_lens[0], span_places)
    ctx_req, ctx_pos = context_places(ctx_lens[0], ctx_index)
    normed = rms_norm(tokens.astype(jnp.float32), input_gain).astype(jnp.bfloat16)
    query = jnp.dot(normed, w_query, preferred_element_type=jnp.float32)
    key_proj = jnp.dot(normed, w_key, preferred_element_type=jnp.float32)
    value_proj = jnp.dot(normed, w_value, preferred_element_type=jnp.float32).astype(jnp.bfloat16)
    query_heads = w_query.shape[1] // head_dim
    kv_local = w_key.shape[1] // head_dim
    group = query_heads // kv_local
    queries = rotate(
        rms_norm(query.reshape(tok_count, query_heads, head_dim), q_gain), query_pos
    ).astype(jnp.bfloat16)
    queries = queries.reshape(tok_count, kv_local, group, head_dim).transpose(1, 2, 0, 3)
    span_keys = rotate(
        rms_norm(key_proj.reshape(tok_count, kv_local, head_dim), k_gain), query_pos
    ).astype(jnp.bfloat16)
    all_keys = jnp.concatenate(
        [ctx_key[0], span_keys.reshape(tok_count, kv_local * head_dim)], axis=0
    )
    all_values = jnp.concatenate([ctx_value[0], value_proj], axis=0)
    key_req = jnp.concatenate([ctx_req, query_req], axis=0)
    key_pos = jnp.concatenate([ctx_pos, query_pos], axis=0)
    scale = 1.0 / math.sqrt(head_dim)
    start_state = (
        jnp.full((kv_local, group, tok_count), -1e30, jnp.float32),
        jnp.zeros((kv_local, group, tok_count), jnp.float32),
        jnp.zeros((kv_local, group, tok_count, head_dim), jnp.float32),
    )
    state = start_state
    piece_keys = lax.all_gather(all_keys, "seq", axis=0, tiled=True)
    piece_values = lax.all_gather(all_values, "seq", axis=0, tiled=True)
    piece_req = lax.all_gather(key_req, "seq", axis=0, tiled=True)
    piece_pos = lax.all_gather(key_pos, "seq", axis=0, tiled=True)
    length = piece_keys.shape[0]
    block = length
    for candidate in (2048, 1280, 1024, 640, 512):
        if length > candidate and length % candidate == 0:
            block = candidate
            break
    count = length // block

    def advance(running, items):
        block_keys, block_values, block_req, block_pos = items
        key_heads = block_keys.reshape(block, kv_local, head_dim)
        value_heads = block_values.reshape(block, kv_local, head_dim)
        visible = (query_req[:, None] == block_req[None, :]) & (
            block_pos[None, :] <= query_pos[:, None]
        )
        largest, total, accum = running
        scores = (
            jnp.einsum("hgtd,khd->hgtk", queries, key_heads, preferred_element_type=jnp.float32)
            * scale
        )
        scores = jnp.where(visible[None, None], scores, -jnp.inf)
        new_largest = jnp.maximum(largest, jnp.max(scores, axis=-1))
        expo = jnp.exp(scores - new_largest[..., None])
        factor = jnp.exp(largest - new_largest)
        total = factor * total + jnp.sum(expo, axis=-1)
        accum = factor[..., None] * accum + jnp.einsum(
            "hgtk,khd->hgtd",
            expo.astype(jnp.bfloat16),
            value_heads,
            preferred_element_type=jnp.float32,
        )
        running = (new_largest, total, accum)
        return (running, None)

    stacked = (
        piece_keys.reshape(count, block, -1),
        piece_values.reshape(count, block, -1),
        piece_req.reshape(count, block),
        piece_pos.reshape(count, block),
    )
    state, _ = lax.scan(advance, state, stacked)
    largest, total, accum = state
    attn = (
        (accum / total[..., None])
        .transpose(2, 0, 1, 3)
        .reshape(tok_count, query_heads * head_dim)
        .astype(jnp.bfloat16)
    )
    half = tok_count // lax.axis_size("tp")
    proj = lax.psum_scatter(
        jnp.dot(attn, w_out, preferred_element_type=jnp.float32).astype(jnp.bfloat16),
        "tp",
        scatter_dimension=0,
        tiled=True,
    ).astype(jnp.float32)
    own_rows = lax.dynamic_slice_in_dim(tokens, lax.axis_index("tp") * half, half, 0)
    resid = (own_rows.astype(jnp.float32) + proj).astype(jnp.bfloat16)
    mixed = rms_norm(resid.astype(jnp.float32), post_gain).astype(jnp.bfloat16)
    top = route_ids.shape[2]
    row_ids = route_ids[0].reshape(-1)
    row_count = row_ids.shape[0]
    seq_tp = lax.axis_size("seq") * lax.axis_size("tp")
    pd_count = lax.axis_size("pd")
    device_count = seq_tp * pd_count
    exp_local = w_gate_up.shape[0]
    experts = device_count * exp_local
    capacity = max(2, 3 * tok_count * top // (2 * lax.axis_size("tp") * experts))
    picks = (row_ids[:, None] == jnp.arange(experts, dtype=jnp.int32)[None, :]).astype(jnp.bfloat16)
    earlier = (
        lax.broadcasted_iota(jnp.int32, (row_count, row_count), 0)
        > lax.broadcasted_iota(jnp.int32, (row_count, row_count), 1)
    ).astype(jnp.bfloat16)
    before = jnp.dot(earlier, picks, preferred_element_type=jnp.float32)
    rank = jnp.sum(before * picks.astype(jnp.float32), axis=1).astype(jnp.int32)
    target = row_ids * capacity + rank
    row_token = jnp.arange(row_count, dtype=jnp.int32) // top
    outgoing = jnp.zeros((experts * capacity, width), jnp.bfloat16).at[target].set(mixed[row_token])
    outgoing = outgoing.reshape(device_count, exp_local, capacity, width)
    returned = lax.all_to_all(
        expert_mlp(
            lax.all_to_all(outgoing, ("seq", "tp", "pd"), split_axis=0, concat_axis=0, tiled=True),
            w_gate_up,
            w_down,
        ),
        ("seq", "tp", "pd"),
        split_axis=0,
        concat_axis=0,
        tiled=True,
    )
    gathered = returned.reshape(experts * capacity, width)[target]
    weights = route_weights[0]
    weights = weights / jnp.sum(weights, axis=-1, keepdims=True)
    moe = jnp.einsum(
        "tkd,tk->td",
        gathered.reshape(half, top, width),
        weights,
        preferred_element_type=jnp.float32,
    )
    layer_out = (resid.astype(jnp.float32) + moe).astype(jnp.bfloat16)[None]
    layers = earlier_kv.shape[0]
    per_device = tok_count // PAGE
    page_count = layers * per_device
    seq_size = lax.axis_size("seq")
    page_cap = max(1, page_count // seq_size)
    pages = earlier_kv[:, 0].reshape(layers, per_device, PAGE, kv_local, 2 * head_dim)
    pages = pages.transpose(3, 0, 1, 2, 4).reshape(kv_local, page_count, PAGE, 2 * head_dim)
    table = page_table[:, 0].transpose(2, 0, 1).reshape(kv_local, page_count)
    owners = table // page_count
    slots = table % page_count
    order = jnp.arange(page_count, dtype=jnp.int32)
    same = (owners[:, :, None] == owners[:, None, :]) & (
        order[None, None, :] < order[None, :, None]
    )
    page_rank = jnp.sum(same.astype(jnp.int32), axis=2)
    page_target = owners * page_cap + page_rank
    head_rows = jnp.broadcast_to(jnp.arange(kv_local, dtype=jnp.int32)[:, None], page_target.shape)
    outgoing_pages = (
        jnp.zeros((kv_local, seq_size * page_cap, PAGE, 2 * head_dim), jnp.bfloat16)
        .at[head_rows, page_target]
        .set(pages)
    )
    outgoing_slots = (
        jnp.full((kv_local, seq_size * page_cap), -1, jnp.int32)
        .at[head_rows, page_target]
        .set(slots)
    )
    arrived_pages, arrived_slots = (
        lax.all_to_all(outgoing_pages, "seq", split_axis=1, concat_axis=1, tiled=True),
        lax.all_to_all(outgoing_slots, "seq", split_axis=1, concat_axis=1, tiled=True),
    )
    placing = (arrived_slots[:, None, :] == order[None, :, None]).astype(jnp.bfloat16)
    cache = jnp.einsum(
        "hkr,hrpc->hkpc", placing, arrived_pages, preferred_element_type=jnp.float32
    ).astype(jnp.bfloat16)
    decode_cache = cache[None, :, None]
    return (layer_out, decode_cache)


def solution(mesh):
    in_specs = (
        P("pd", "seq", None),
        P(),
        P(None, "tp"),
        P(None, "tp"),
        P(None, "tp"),
        P(),
        P(),
        P("tp", None),
        P(),
        P("pd", "seq", "tp"),
        P("pd", "seq", "tp"),
        P("pd", None),
        P("pd", None),
        P("pd", ("seq", "tp"), None),
        P("pd", ("seq", "tp"), None),
        P(("seq", "tp", "pd"), None, None),
        P(("seq", "tp", "pd"), None, None),
        P(None, "pd", "seq", "tp", None),
        P(None, "pd", "seq", "tp"),
    )
    out_specs = (P("pd", ("seq", "tp"), None), P("seq", "tp", "pd", None, None, None))
    return jax.shard_map(shards, mesh=mesh, in_specs=in_specs, out_specs=out_specs, check_vma=False)
```

profile of v0, /device:TPU:0, one launch (start us, length us, event | category | flops | bytes accessed | tf_op | source)
XLA Modules:
  0.0 561.5 jit_solution(12165041694039212469)
XLA Ops:
  8.9 1.5 fusion.43
  10.5 6.5 %copy.78 = bf16[1024,2048]{1,0:T(8,128)(2,1)} copy(bf16[1024,2048]{0,1:T(8,128)(2,1)} %bitcast.223) | data formatting | bytes 8388608 | tf_op jit(solution)/shard_map/dot_general | solution.py:90
  17.0 3.9 multiply_reduce_fusion
  22.6 2.0 copy.63
  24.7 1.9 multiply_reduce_fusion.1
  27.4 35.7 %all_gather.14 = bf16[2560,128]{1,0:T(8,128)(2,1)} all-gather(bf16[320,128]{1,0:T(8,128)(2,1)S(1)} %copy.61), channel_id=1, replica_groups=mesh['seq'=8,'tp'=2,'pd'=2] {'seq'}, dimensions={0}, use_global_device_ids=true | all-gather | bytes 737280 | tf_op jit(solution)/shard_map/all_gather | solution.py:116
  65.1 37.1 %all-reduce.3 = (s32[2560]{0:T(1024)S(1)}, s32[2560]{0:T(1024)S(1)}) all-reduce(s32[2560]{0:T(1024)S(1)} %add_dynamic-update-slice_fusion, s32[2560]{0:T(1024)S(1)} %add_dynamic-update-slice_fusion.1), channel_id=1, replica_groups=mesh['seq'=8,'tp'=2,'pd'=2] {'seq'}, use_global_device_ids=true, to_apply=%add.1 | all-reduce | flops 5120 | bytes 40960
  102.3 1.9 convolution_convert_fusion.2
  104.1 34.2 %all_gather.15 = bf16[2560,128]{1,0:T(8,128)(2,1)} all-gather(bf16[320,128]{1,0:T(8,128)(2,1)S(1)} %pad_maximum_fusion), channel_id=1, replica_groups=mesh['seq'=8,'tp'=2,'pd'=2] {'seq'}, dimensions={0}, use_global_device_ids=true | all-gather | bytes 737280 | tf_op jit(solution)/shard_map/all_gather | solution.py:117
  138.4 35.8 %while.15 = (s32[]{:T(128)}, f32[1,8,256]{2,1,0:T(8,128)S(1)}, f32[1,8,256]{2,1,0:T(8,128)S(1)}, f32[1,8,256,128]{3,2,1,0:T(8,128)}, s32[256]{0:T(256)S(1)}, /*i...) while((s32[]{:T(128)}, f32[1,8,256]{2,1,0:T(8,128)S(1)}, ...), condition=%wide.region_13.14_spmd.clone, body=%wide.region_10.13_spmd.clone.sunk | while | flops 1372794880 | bytes 78152872 | solution.py:160
  139.3 6.7 %fusion.111 = (f32[8,256]{1,0:T(8,128)S(1)}, f32[1280,8,256]{2,0,1:T(8,128)}) fusion(pred[256,1280]{0,1:T(8,128)(4,1)S(1)} %compare_and_fusion.2, bf16[1,8,256,128]{3,2,1,0:T(8,128)(2,1)} %get-tuple-element.310, bf16[2,1280,128]{2,1,0:T(8,128)(2,1)} %get-tuple-element.309, s32[]{:T(128)} %get-tuple-element.288), kind=kOutput, calls=%fused_computation.9.clone.1 | convolution fusion | flops 678950912 | bytes 11674112 | tf_op jit(solution)/shard_map/while/body/eval_jaxpr/hgtd,khd->hgtk/dot_general | solution.py:137
  146.1 7.8 %fusion.114 = f32[1,8,256,128]{3,2,1,0:T(8,128)} fusion(f32[1280,8,256]{2,0,1:T(8,128)} %get-tuple-element.273, f32[8,256]{1,0:T(8,128)S(1)} %bitcast.225, pred[256,1280]{0,1:T(8,128)(4,1)S(1)} %compare_and_fusion.2, f32[1,8,256,128]{3,2,1,0:T(8,128)} %get-tuple-element.291, f32[8,256]{1,0:T(8,128)S(1)} %get-tuple-element.274, pred[]{:T(512)S(6)} %compare.45, ...), kind=kOutput, calls=%fused_computation.13.clone.1 | convolution fusion | flops 682360832 | bytes 13255169 | tf_op jit(solution)/shard_map/while/body/eval_jaxpr/hgtk,khd->hgtd/dot_general | solution.py:145
  153.9 2.1 fusion.113
  157.1 6.7 %fusion.111 = (f32[8,256]{1,0:T(8,128)S(1)}, f32[1280,8,256]{2,0,1:T(8,128)}) fusion(pred[256,1280]{0,1:T(8,128)(4,1)S(1)} %compare_and_fusion.2, bf16[1,8,256,128]{3,2,1,0:T(8,128)(2,1)} %get-tuple-element.310, bf16[2,1280,128]{2,1,0:T(8,128)(2,1)} %get-tuple-element.309, s32[]{:T(128)} %get-tuple-element.288), kind=kOutput, calls=%fused_computation.9.clone.1 | convolution fusion | flops 678950912 | bytes 11674112 | tf_op jit(solution)/shard_map/while/body/eval_jaxpr/hgtd,khd->hgtk/dot_general | solution.py:137
  163.8 8.2 %fusion.114 = f32[1,8,256,128]{3,2,1,0:T(8,128)} fusion(f32[1280,8,256]{2,0,1:T(8,128)} %get-tuple-element.273, f32[8,256]{1,0:T(8,128)S(1)} %bitcast.225, pred[256,1280]{0,1:T(8,128)(4,1)S(1)} %compare_and_fusion.2, f32[1,8,256,128]{3,2,1,0:T(8,128)} %get-tuple-element.291, f32[8,256]{1,0:T(8,128)S(1)} %get-tuple-element.274, pred[]{:T(512)S(6)} %compare.45, ...), kind=kOutput, calls=%fused_computation.13.clone.1 | convolution fusion | flops 682360832 | bytes 13255169 | tf_op jit(solution)/shard_map/while/body/eval_jaxpr/hgtk,khd->hgtd/dot_general | solution.py:145
  172.0 2.1 fusion.113
  174.2 2.6 copy.64
  178.1 4.4 convolution_convert_fusion
  184.4 3.5 all-to-all-start.2
  192.2 24.5 %scatter_custom_fusion = bf16[1536,2048]{1,0:T(8,128)(2,1)} fusion(s32[1024]{0:T(1024)S(1)} %bitcast.233, bf16[128,2048]{1,0:T(8,128)(2,1)} %fusion.53, s32[1024]{0:T(1024)S(1)} %broadcast_clamp_fusion.1, bf16[]{:T(256)} %constant.111.clone.1), kind=kCustom, calls=%fused_computation.42 | custom fusion | bytes 6291968 | tf_op jit(solution)/shard_map/scatter | solution.py:196
  216.8 6.2 %all-to-all-start = ((bf16[32,1,48,2048]{3,2,1,0:T(8,128)(2,1)}), bf16[32,1,48,2048]{3,2,1,0:T(8,128)(2,1)}, u32[]{:S(2)}, u32[]{:S(2)}) async-start(bf16[32,1,48,2048]{3,2,1,0:T(8,128)(2,1)} %bitcast.220), calls=%async_computation.1 | async-start | bytes 12582912 | tf_op jit(solution)/shard_map/all_to_all | solution.py:200
  224.1 3.4 scatter_fusion
  227.4 135.7 %all-to-all-done = bf16[32,1,48,2048]{3,2,1,0:T(8,128)(2,1)} async-done(((bf16[32,1,48,2048]{3,2,1,0:T(8,128)(2,1)}), bf16[32,1,48,2048]{3,2,1,0:T(8,128)(2,1)}, u32[]{:S(2)}, u32[]{:S(2)}) %all-to-all-start) | async-done | bytes 6291488 | tf_op jit(solution)/shard_map/all_to_all | solution.py:200
  363.2 4.2 all-to-all-start.3
  367.4 14.2 %fusion.26 = f32[32,1,48,1536]{3,2,0,1:T(8,128)S(1)} fusion(bf16[1,2048,1536]{2,1,0:T(8,128)(2,1)} %param.36, bf16[32,1,48,2048]{3,2,1,0:T(8,128)(2,1)} %all-to-all-done), kind=kOutput, calls=%fused_computation.37 | convolution fusion | flops 9663676416 | bytes 22020096 | tf_op jit(solution)/shard_map/sejd,edf->sejf/dot_general | solution.py:50
  381.6 7.0 %convert_bitcast_fusion = bf16[32,1,48,2048]{3,2,1,0:T(8,128)(2,1)} fusion(bf16[1,768,2048]{2,1,0:T(8,128)(2,1)S(1)} %copy-done, f32[32,1,48,1536]{3,2,0,1:T(8,128)S(1)} %fusion.26), kind=kOutput, calls=%fused_computation.36 | convolution fusion | flops 4842061824 | bytes 18874368 | tf_op jit(solution)/shard_map/sejf,efd->sejd/dot_general | solution.py:53
  388.6 4.7 all-to-all-done.3
  393.3 3.9 all-to-all-start.1
  398.6 1.9 fusion.48
  401.8 135.5 %all-to-all-done.1 = bf16[32,1,48,2048]{3,2,1,0:T(8,128)(2,1)} async-done(((bf16[32,1,48,2048]{3,2,1,0:T(8,128)(2,1)}), bf16[32,1,48,2048]{3,2,1,0:T(8,128)(2,1)}, u32[]{:S(2)}, u32[]{:S(2)}) %all-to-all-start.1) | async-done | bytes 6291488 | tf_op jit(solution)/shard_map/all_to_all | solution.py:198
  537.3 12.4 %gather_fusion = bf16[1024,2048]{1,0:T(8,128)(2,1)} fusion(bf16[1536,2048]{1,0:T(8,128)(2,1)} %bitcast.48, s32[1024]{0:T(1024)S(1)} %broadcast_clamp_fusion), kind=kCustom, calls=%fused_computation.1 | custom fusion | bytes 8392704 | tf_op jit(solution)/shard_map/gather | solution.py:209
  549.8 3.5 fusion.32
  (118 shorter events, 19.8 us)
Async XLA Ops:
  7.2 374.4 %copy-start = (bf16[1,768,2048]{2,1,0:T(8,128)(2,1)S(1)}, bf16[1,768,2048]{2,1,0:T(8,128)(2,1)}, u32[]{:S(2)}) copy-start(bf16[1,768,2048]{2,1,0:T(8,128)(2,1)} %param.37) | copy-start | bytes 9437188
  7.2 181.8 %reduce-scatter.2.cloned.1.call-start = ((), (), s32[]{:S(2)}) async-start(), calls=%async_computation.5 | async-start | bytes 1572864 | tf_op jit(solution)/shard_map/reduce_scatter | solution.py:169
  10.4 6.5 %copy-start.13 = (f32[2048]{0:T(1024)S(1)}, f32[2048]{0:T(1024)}, u32[]{:S(2)}) copy-start(f32[2048]{0:T(1024)} %param.22) | copy-start | bytes 24580
  17.0 4.0 copy-start.12
  17.0 4.4 copy-start.10
  20.9 5.8 %copy-start.11 = (f32[128]{0:T(128)S(1)}, f32[128]{0:T(128)}, u32[]{:S(2)}) copy-start(f32[128]{0:T(128)} %param.27) | copy-start | bytes 1540
  21.4 5.7 %copy-start.4 = (bf16[1,64,128]{2,1,0:T(8,128)(2,1)S(1)}, bf16[1,64,128]{2,1,0:T(8,128)(2,1)}, u32[]{:S(2)}) copy-start(bf16[1,64,128]{2,1,0:T(8,128)(2,1)} %param.30) | copy-start | bytes 49156
  21.6 41.9 %copy-start.14 = (u32[32]{0:T(128)S(1)}, u32[32]{0:T(128)}, u32[]{:S(2)}) copy-start(u32[32]{0:T(128)} %constant.142) | copy-start | bytes 388
  21.8 82.3 %copy-start.5 = (bf16[1,64,128]{2,1,0:T(8,128)(2,1)S(1)}, bf16[1,64,128]{2,1,0:T(8,128)(2,1)}, u32[]{:S(2)}) copy-start(bf16[1,64,128]{2,1,0:T(8,128)(2,1)} %param.31) | copy-start | bytes 49156
  146.1 7.8 %copy-start.1 = (f32[1280,8,256]{2,0,1:T(8,128)S(1)}, f32[1280,8,256]{2,0,1:T(8,128)}, u32[]{:S(2)}) copy-start(f32[1280,8,256]{2,0,1:T(8,128)} %get-tuple-element.273) | copy-start | bytes 31457284 | tf_op jit(solution)/shard_map/while
  163.8 8.2 %copy-start.1 = (f32[1280,8,256]{2,0,1:T(8,128)S(1)}, f32[1280,8,256]{2,0,1:T(8,128)}, u32[]{:S(2)}) copy-start(f32[1280,8,256]{2,0,1:T(8,128)} %get-tuple-element.273) | copy-start | bytes 31457284 | tf_op jit(solution)/shard_map/while
  178.0 4.5 copy-start.9
  178.1 9.9 %copy-start.6 = (s32[1,128,8]{1,2,0:T(8,128)S(1)}, s32[1,128,8]{1,2,0:T(8,128)}, u32[]{:S(2)}) copy-start(s32[1,128,8]{1,2,0:T(8,128)} %param.34) | copy-start | bytes 12292
  178.1 13.1 %copy-start.8 = (f32[2048]{0:T(1024)S(1)}, f32[2048]{0:T(1024)}, u32[]{:S(2)}) copy-start(f32[2048]{0:T(1024)} %param.29) | copy-start | bytes 24580
  184.4 32.3 %all-to-all-start.2 = ((s32[1,8,2]{2,0,1:T(1,128)}), s32[1,8,2]{2,0,1:T(1,128)S(1)}, u32[]{:S(2)}, u32[]{:S(2)}) async-start(s32[1,8,2]{2,0,1:T(1,128)} %bitcast.58), calls=%async_computation.3 | async-start | bytes 8192 | tf_op jit(solution)/shard_map/all_to_all | solution.py:248
  190.4 0.8 copy-start.2
  216.8 146.4 %all-to-all-start = ((bf16[32,1,48,2048]{3,2,1,0:T(8,128)(2,1)}), bf16[32,1,48,2048]{3,2,1,0:T(8,128)(2,1)}, u32[]{:S(2)}, u32[]{:S(2)}) async-start(bf16[32,1,48,2048]{3,2,1,0:T(8,128)(2,1)} %bitcast.220), calls=%async_computation.1 | async-start | bytes 12582912 | tf_op jit(solution)/shard_map/all_to_all | solution.py:200
  363.2 30.1 %all-to-all-start.3 = ((bf16[1,16,128,256]{3,2,0,1:T(8,128)(2,1)}), bf16[1,16,128,256]{3,2,0,1:T(8,128)(2,1)}, u32[]{:S(2)}, u32[]{:S(2)}) async-start(bf16[1,16,128,256]{3,2,0,1:T(8,128)(2,1)} %bitcast.221), calls=%async_computation.4 | async-start | bytes 2097152 | tf_op jit(solution)/shard_map/all_to_all | solution.py:247
  388.6 8.6 %copy-start.7 = (f32[1,128,8]{1,2,0:T(8,128)S(1)}, f32[1,128,8]{1,2,0:T(8,128)}, u32[]{:S(2)}) copy-start(f32[1,128,8]{1,2,0:T(8,128)} %param.35) | copy-start | bytes 12292
  393.3 144.1 %all-to-all-start.1 = ((bf16[32,1,48,2048]{3,2,1,0:T(8,128)(2,1)}), bf16[32,1,48,2048]{3,2,1,0:T(8,128)(2,1)}, u32[]{:S(2)}, u32[]{:S(2)}) async-start(bf16[32,1,48,2048]{3,2,1,0:T(8,128)(2,1)} %convert_bitcast_fusion), calls=%async_computation.2 | async-start | bytes 12582912 | tf_op jit(solution)/shard_map/all_to_all | solution.py:198
  549.8 3.5 copy-start.3
Sparse Core Ops, SparseCore 0:
  182.7 5.8 reduce-scatter.1
where the time goes:
time: 567 us; the launch traced here: 561 us
  waiting for transfers between devices  276 us (49%)
  blocking collectives  107 us (19%)
  matrix products  68.7 us (12%)
  local copies, waits for them, and re-layouts  58.3 us (10%)
  other arithmetic  18.1 us (3%)
  starting transfers between devices  17.8 us (3%)
  between operations  15.5 us (3%)
    all_to_all x1, waiting for transfers between devices, shards(): lax.all_to_all(outgoing, ('seq', 'tp', 'pd'), split_axis=0, concat_axis=0...  136 us
    all_to_all x1, waiting for transfers between devices, shards(): lax.all_to_all(expert_mlp(lax.all_to_all(outgoing, ('seq', 'tp', 'pd'), s...  136 us
    unnamed x1, blocking collectives  37.1 us
    all_gather x1, blocking collectives, shards(): piece_keys = lax.all_gather(all_keys, 'seq', axis=0, tiled=True)  35.7 us
    all_gather x1, blocking collectives, shards(): piece_values = lax.all_gather(all_values, 'seq', axis=0, tiled=True)  34.2 us
    scatter x1, local copies, waits for them, and re-layouts, shards(): jnp.zeros((experts * capacity, width), jnp.bfloat16).at[target]  24.5 us
    dot_general x2, matrix products, advance(): jnp.einsum('hgtk,khd->hgtd', expo.astype(jnp.bfloat16), value_heads, pref...  16 us
    dot_general x1, matrix products, expert_mlp(): jnp.einsum('sejd,edf->sejf', arrived, w_gate_up, preferred_element_type=j...  14.2 us
  transfers between devices with their start and end apart: 5, of which 3 were waited for; matrix products, arithmetic and copies ran while one was open for 11% of the time, Pallas kernels for 0%

commit v1 on v0

--- a/solution.py
+++ b/solution.py
@@ -1,11 +1,356 @@
+import functools
 import math
 
 import jax
 import jax.numpy as jnp
 from jax import lax
+from jax.experimental import pallas as pl
+from jax.experimental.pallas import tpu as pltpu
 from jax.sharding import PartitionSpec as P
 
 PAGE = 128
+MESH = pl.DeviceIdType.MESH
+DEPTH = 4
+
+
+def remote(src, dst, send, recv, device):
+    return pltpu.make_async_remote_copy(
+        src_ref=src,
+        dst_ref=dst,
+        send_sem=send,
+        recv_sem=recv,
+        device_id=device,
+        device_id_type=MESH,
+    )
+
+
+def position():
+    seq = lax.axis_index("seq")
+    return seq, seq // 2, seq % 2, lax.axis_index("pd"), lax.axis_index("tp")
+
+
+def greet(full):
+    seq, mz, mx, my, mc = position()
+    barrier = pltpu.get_barrier_semaphore()
+
+    @pl.when(mz > 0)
+    def _():
+        pl.semaphore_signal(barrier, inc=1, device_id={"seq": seq - 2}, device_id_type=MESH)
+
+    @pl.when(mz < DEPTH - 1)
+    def _():
+        pl.semaphore_signal(barrier, inc=1, device_id={"seq": seq + 2}, device_id_type=MESH)
+
+    others = [{"seq": mz * 2 + 1 - mx}]
+    if full:
+        others += [{"pd": 1 - my}, {"tp": 1 - mc}]
+    for other in others:
+        pl.semaphore_signal(barrier, inc=1, device_id=other, device_id_type=MESH)
+    ends = (mz > 0).astype(jnp.int32) + (mz < DEPTH - 1).astype(jnp.int32)
+    pl.semaphore_wait(barrier, len(others) + ends)
+
+
+def gather_kernel(full, in_ref, out_ref, lsem, zu, zd, zr, xs, xr, ys, yr, es, er, fs, fr, cs, cr):
+    seq, mz, mx, my, mc = position()
+    half = in_ref.shape[0] // 2
+    xdev, ydev, cdev = {"seq": mz * 2 + 1 - mx}, {"pd": 1 - my}, {"tp": 1 - mc}
+
+    def slot(o, x, y):
+        return out_ref.at[o, x, y, mc] if full else out_ref.at[o, x]
+
+    def core_slot(o, x, y, c):
+        return out_ref.at[o, x, y, c]
+
+    first, second = pl.ds(0, half), pl.ds(half, half)
+    own = pltpu.make_async_copy(in_ref, slot(mz, mx, my), lsem)
+
+    def zup(src, o):
+        return remote(src, slot(o, mx, my), zu.at[o], zr.at[o], {"seq": seq + 2})
+
+    def zdown(src, o):
+        return remote(src, slot(o, mx, my), zd.at[o], zr.at[o], {"seq": seq - 2})
+
+    def xcopy(src, o, x):
+        return remote(src, slot(o, x, my), xs.at[o], xr.at[o], xdev)
+
+    def ycopy(src, o, y):
+        return remote(src, slot(o, mx, y), ys.at[o], yr.at[o], ydev)
+
+    def ecopy(o, x, y):
+        part = slot(o, x, y).at[first]
+        return remote(part, part, es.at[o], er.at[o], ydev)
+
+    def fcopy(o, x, y):
+        part = slot(o, x, y).at[second]
+        return remote(part, part, fs.at[o], fr.at[o], xdev)
+
+    def ccopy(src, o, x, y, c):
+        k = o * 4 + x * 2 + y
+        return remote(src, core_slot(o, x, y, c), cs.at[k], cr.at[k], cdev)
+
+    def have_z(o, src, up, down):
+        if up:
+
+            @pl.when(mz < DEPTH - 1)
+            def _():
+                zup(src, o).start()
+
+        if down:
+
+            @pl.when(mz > 0)
+            def _():
+                zdown(src, o).start()
+
+        xcopy(src, o, mx).start()
+        if full:
+            ycopy(src, o, my).start()
+            ccopy(src, o, mx, my, mc).start()
+
+    def have_xy(o):
+        xcopy(slot(o, 1 - mx, my), o, 1 - mx).wait_recv()
+        if full:
+            ecopy(o, 1 - mx, my).start()
+            ccopy(slot(o, 1 - mx, my), o, 1 - mx, my, mc).start()
+            ycopy(slot(o, mx, 1 - my), o, 1 - my).wait_recv()
+            fcopy(o, mx, 1 - my).start()
+            ccopy(slot(o, mx, 1 - my), o, mx, 1 - my, mc).start()
+
+    def have_diagonal(o):
+        if full:
+            ecopy(o, 1 - mx, 1 - my).wait_recv()
+            fcopy(o, 1 - mx, 1 - my).wait_recv()
+            ccopy(slot(o, 1 - mx, 1 - my), o, 1 - mx, 1 - my, mc).start()
+
+    def each(step, action):
+        if step == 0:
+            action(mz)
+        elif step > 0:
+            pl.when(mz - step >= 0)(lambda: action(mz - step))
+            pl.when(mz + step < DEPTH)(lambda: action(mz + step))
+
+    greet(full)
+    have_z(mz, in_ref, True, True)
+    own.start()
+    for step in range(1, DEPTH):
+
+        @pl.when(mz - step >= 0)
+        def _():
+            o = mz - step
+            zup(slot(o, mx, my), o).wait_recv()
+            have_z(o, slot(o, mx, my), True, False)
+
+        @pl.when(mz + step < DEPTH)
+        def _():
+            o = mz + step
+            zup(slot(o, mx, my), o).wait_recv()
+            have_z(o, slot(o, mx, my), False, True)
+
+        each(step - 1, have_xy)
+        each(step - 2, have_diagonal)
+    each(DEPTH - 1, have_xy)
+    each(DEPTH - 2, have_diagonal)
+    each(DEPTH - 1, have_diagonal)
+    for o in range(DEPTH):
+        block = slot(o, mx, my)
+        pl.when((mz < DEPTH - 1) & (mz >= o))(lambda: zup(block, o).wait_send())
+        pl.when((mz > 0) & (mz <= o))(lambda: zdown(block, o).wait_send())
+        xcopy(block, o, mx).wait_send()
+        if full:
+            ycopy(block, o, my).wait_send()
+            ecopy(o, 1 - mx, my).wait_send()
+            fcopy(o, mx, 1 - my).wait_send()
+            for x in range(2):
+                for y in range(2):
+                    done = ccopy(slot(o, x, y), o, x, y, 1 - mc)
+                    done.wait_recv()
+                    done.wait_send()
+    own.wait()
+
+
+def gather(block, full, collective_id):
+    shape = (DEPTH, 2, 2, 2) if full else (DEPTH, 2)
+    dma = pltpu.SemaphoreType.DMA
+    return pl.pallas_call(
+        functools.partial(gather_kernel, full),
+        out_shape=jax.ShapeDtypeStruct(shape + block.shape, block.dtype),
+        in_specs=[pl.BlockSpec(memory_space=pl.ANY)],
+        out_specs=pl.BlockSpec(memory_space=pl.ANY),
+        scratch_shapes=[dma] + [dma((DEPTH,))] * 11 + [dma((4 * DEPTH,))] * 2,
+        compiler_params=pltpu.CompilerParams(collective_id=collective_id, has_side_effects=True),
+        name="gather_full" if full else "gather_seq",
+    )(block)
+
+
+def combine_kernel(
+    part_ref, resid_ref, out_ref, s, cb, dx, dy, xb, yb, zub, zdb,
+    ls, cs, cr, dxs, dxr, dys, dyr, xs, xr, ys, yr, zs, zur, zdr,
+):
+    seq, mz, mx, my, mc = position()
+    rows = resid_ref.shape[0]
+    half = rows // 2
+    xdev, ydev, cdev = {"seq": mz * 2 + 1 - mx}, {"pd": 1 - my}, {"tp": 1 - mc}
+    first, second = pl.ds(0, half), pl.ds(half, half)
+    step_rows = 16
+    lower = mz < 2
+    far = jnp.where(lower, 3, 0)
+    order = [
+        far,
+        jnp.where(mz == 0, 2, jnp.where(mz == 1, 0, jnp.where(mz == 2, 3, 1))),
+        jnp.where((mz == 0) | (mz == 2), 1, 2),
+        mz,
+    ]
+    middle = (mz == 1) | (mz == 2)
+
+    def load(o, x, y):
+        return pltpu.make_async_copy(
+            part_ref.at[o, x, y, mc], s.at[o, x, y], ls.at[o * 4 + x * 2 + y]
+        )
+
+    def core(o, x, y):
+        k = o * 4 + x * 2 + y
+        return remote(part_ref.at[o, x, y, 1 - mc], cb.at[o, x, y], cs.at[k], cr.at[k], cdev)
+
+    def diag_x(o):
+        return remote(s.at[o, 1 - mx, 1 - my].at[first], dx.at[o], dxs.at[o], dxr.at[o], xdev)
+
+    def diag_y(o):
+        return remote(s.at[o, 1 - mx, 1 - my].at[second], dy.at[o], dys.at[o], dyr.at[o], ydev)
+
+    def send_x(o):
+        return remote(s.at[o, 1 - mx, my], xb.at[o], xs.at[o], xr.at[o], xdev)
+
+    def send_y(o):
+        return remote(s.at[o, mx, 1 - my], yb.at[o], ys.at[o], yr.at[o], ydev)
+
+    def send_up(o):
+        return remote(s.at[o, mx, my], zub.at[o], zs.at[o], zur.at[o], {"seq": seq + 2})
+
+    def send_down(o):
+        return remote(s.at[o, mx, my], zdb.at[o], zs.at[o], zdr.at[o], {"seq": seq - 2})
+
+    def add(target, start, count, *others):
+        @pl.loop(0, count // step_rows)
+        def _(i):
+            at = pl.ds(pl.multiple_of(start + i * step_rows, step_rows), step_rows)
+            total = target[at, :].astype(jnp.float32)
+            for other in others:
+                there = pl.ds(pl.multiple_of(i * step_rows, step_rows), step_rows)
+                total = total + other[there, :].astype(jnp.float32)
+            target[at, :] = total.astype(target.dtype)
+
+    def begin(o):
+        for x, y in ((1 - mx, 1 - my), (1 - mx, my), (mx, 1 - my), (mx, my)):
+            core(o, x, y).start()
+            load(o, x, y).start()
+
+    def stage_a(o):
+        for x, y in ((1 - mx, 1 - my), (1 - mx, my), (mx, 1 - my), (mx, my)):
+            load(o, x, y).wait()
+            core(o, x, y).wait_recv()
+            add(s.at[o, x, y], 0, rows, cb.at[o, x, y])
+            if x is not mx and y is not my:
+                diag_x(o).start()
+                diag_y(o).start()
+
+    def stage_b(o):
+        diag_x(o).wait_recv()
+        add(s.at[o, mx, 1 - my], 0, half, dx.at[o])
+        send_y(o).start()
+        diag_y(o).wait_recv()
+        add(s.at[o, 1 - mx, my], half, half, dy.at[o])
+        send_x(o).start()
+
+    def pass_on(o, incoming):
+        up = o > mz
+
+        @pl.when(up)
+        def _():
+            if incoming:
+                send_up(o).wait_recv()
+                add(s.at[o, mx, my], 0, rows, zub.at[o])
+            send_up(o).start()
+
+        @pl.when(jnp.logical_not(up))
+        def _():
+            if incoming:
+                send_down(o).wait_recv()
+                add(s.at[o, mx, my], 0, rows, zdb.at[o])
+            send_down(o).start()
+
+    def stage_c(j):
+        o = order[j]
+        send_x(o).wait_recv()
+        send_y(o).wait_recv()
+        add(s.at[o, mx, my], 0, rows, xb.at[o], yb.at[o])
+        if j < DEPTH - 1:
+            pl.when(jnp.logical_not(middle))(lambda: pass_on(o, False))
+        for late in {0: (), 1: (0,), 2: (1, 2), 3: ()}[j]:
+            pl.when(middle)(lambda: pass_on(order[late], True))
+
+    greet(True)
+    for o in order:
+        begin(o)
+    for t in range(DEPTH + 2):
+        if t < DEPTH:
+            stage_a(order[t])
+        if 1 <= t <= DEPTH:
+            stage_b(order[t - 1])
+        if t >= 2:
+            stage_c(t - 2)
+
+    pl.when(mz > 0)(lambda: send_up(mz).wait_recv())
+    pl.when(mz < DEPTH - 1)(lambda: send_down(mz).wait_recv())
+
+    @pl.loop(0, rows // step_rows)
+    def _(i):
+        at = pl.ds(pl.multiple_of(i * step_rows, step_rows), step_rows)
+        out_ref[at, :] = s[mz, mx, my, at, :].astype(jnp.float32) + resid_ref[at, :].astype(
+            jnp.float32
+        )
+
+    @pl.when(mz > 0)
+    def _():
+        add(out_ref, 0, rows, zub.at[mz])
+
+    @pl.when(mz < DEPTH - 1)
+    def _():
+        add(out_ref, 0, rows, zdb.at[mz])
+
+    for o in range(DEPTH):
+        for x in range(2):
+            for y in range(2):
+                core(o, x, y).wait_send()
+        diag_x(o).wait_send()
+        diag_y(o).wait_send()
+        send_x(o).wait_send()
+        send_y(o).wait_send()
+        pl.when(mz != o)(lambda: send_up(o).wait_send())
+
+
+def combine(partial, resid, collective_id):
+    rows, width = resid.shape
+    dma = pltpu.SemaphoreType.DMA
+    bf16 = jnp.bfloat16
+    vmem = pl.BlockSpec(memory_space=pltpu.VMEM)
+    return pl.pallas_call(
+        combine_kernel,
+        out_shape=jax.ShapeDtypeStruct((rows, width), jnp.float32),
+        in_specs=[pl.BlockSpec(memory_space=pl.ANY), vmem],
+        out_specs=vmem,
+        scratch_shapes=[
+            pltpu.VMEM((DEPTH, 2, 2, rows, width), bf16),
+            pltpu.VMEM((DEPTH, 2, 2, rows, width), bf16),
+            pltpu.VMEM((DEPTH, rows // 2, width), bf16),
+            pltpu.VMEM((DEPTH, rows // 2, width), bf16),
+        ]
+        + [pltpu.VMEM((DEPTH, rows, width), bf16)] * 4
+        + [dma((4 * DEPTH,))] * 3
+        + [dma((DEPTH,))] * 11,
+        compiler_params=pltpu.CompilerParams(
+            collective_id=collective_id, has_side_effects=True, vmem_limit_bytes=48 << 20
+        ),
+        name="combine",
+    )(partial, resid)
 
 
 def rms_norm(values, gain):
@@ -255,6 +600,214 @@
     return (layer_out, decode_cache)
 
 
+def shards_small(
+    hidden_in,
+    input_gain,
+    w_query,
+    w_key,
+    w_value,
+    q_gain,
+    k_gain,
+    w_out,
+    post_gain,
+    ctx_key,
+    ctx_value,
+    span_lens,
+    ctx_lens,
+    route_ids,
+    route_weights,
+    w_gate_up,
+    w_down,
+    earlier_kv,
+    page_table,
+):
+    tokens = hidden_in[0]
+    tok_count = tokens.shape[0]
+    width = tokens.shape[1]
+    ctx_count = ctx_key.shape[1]
+    head_dim = q_gain.shape[0]
+    seq_index = lax.axis_index("seq")
+    span_places = seq_index * tok_count + jnp.arange(tok_count, dtype=jnp.int32)
+    query_req, query_pos = query_places(span_lens[0], ctx_lens[0], span_places)
+    normed = rms_norm(tokens.astype(jnp.float32), input_gain).astype(jnp.bfloat16)
+    query = jnp.dot(normed, w_query, preferred_element_type=jnp.float32)
+    key_proj = jnp.dot(normed, w_key, preferred_element_type=jnp.float32)
+    value_proj = jnp.dot(normed, w_value, preferred_element_type=jnp.float32).astype(jnp.bfloat16)
+    query_heads = w_query.shape[1] // head_dim
+    kv_local = w_key.shape[1] // head_dim
+    group = query_heads // kv_local
+    queries = rotate(
+        rms_norm(query.reshape(tok_count, query_heads, head_dim), q_gain), query_pos
+    ).astype(jnp.bfloat16)
+    queries = queries.reshape(tok_count, kv_local, group, head_dim).transpose(1, 2, 0, 3)
+    span_keys = rotate(
+        rms_norm(key_proj.reshape(tok_count, kv_local, head_dim), k_gain), query_pos
+    ).astype(jnp.bfloat16)
+    all_keys = jnp.concatenate(
+        [ctx_key[0], span_keys.reshape(tok_count, kv_local * head_dim)], axis=0
+    )
+    all_values = jnp.concatenate([ctx_value[0], value_proj], axis=0)
+    scale = 1.0 / math.sqrt(head_dim)
+    start_state = (
+        jnp.full((kv_local, group, tok_count), -1e30, jnp.float32),
+        jnp.zeros((kv_local, group, tok_count), jnp.float32),
+        jnp.zeros((kv_local, group, tok_count, head_dim), jnp.float32),
+    )
+    state = start_state
+    both = gather(jnp.concatenate([all_keys, all_values], axis=1), False, 1)
+    both = both.reshape(-1, 2 * head_dim)
+    piece_keys, piece_values = both[:, :head_dim], both[:, head_dim:]
+    everywhere = jnp.arange(tok_count * lax.axis_size("seq"), dtype=jnp.int32)
+    places_req, places_pos = query_places(span_lens[0], ctx_lens[0], everywhere)
+    all_ctx = jnp.arange(ctx_count * lax.axis_size("seq"), dtype=jnp.int32)
+    prior_req, prior_pos = context_places(ctx_lens[0], all_ctx)
+    shape_ctx, shape_tok = (-1, ctx_count), (-1, tok_count)
+    piece_req = jnp.concatenate(
+        [prior_req.reshape(shape_ctx), places_req.reshape(shape_tok)], axis=1
+    ).reshape(-1)
+    piece_pos = jnp.concatenate(
+        [prior_pos.reshape(shape_ctx), places_pos.reshape(shape_tok)], axis=1
+    ).reshape(-1)
+    length = piece_keys.shape[0]
+    block = length
+    for candidate in (2048, 1280, 1024, 640, 512):
+        if length > candidate and length % candidate == 0:
+            block = candidate
+            break
+    count = length // block
+
+    def advance(running, items):
+        block_keys, block_values, block_req, block_pos = items
+        key_heads = block_keys.reshape(block, kv_local, head_dim)
+        value_heads = block_values.reshape(block, kv_local, head_dim)
+        visible = (query_req[:, None] == block_req[None, :]) & (
+            block_pos[None, :] <= query_pos[:, None]
+        )
+        largest, total, accum = running
+        scores = (
+            jnp.einsum("hgtd,khd->hgtk", queries, key_heads, preferred_element_type=jnp.float32)
+            * scale
+        )
+        scores = jnp.where(visible[None, None], scores, -jnp.inf)
+        new_largest = jnp.maximum(largest, jnp.max(scores, axis=-1))
+        expo = jnp.exp(scores - new_largest[..., None])
+        factor = jnp.exp(largest - new_largest)
+        total = factor * total + jnp.sum(expo, axis=-1)
+        accum = factor[..., None] * accum + jnp.einsum(
+            "hgtk,khd->hgtd",
+            expo.astype(jnp.bfloat16),
+            value_heads,
+            preferred_element_type=jnp.float32,
+        )
+        running = (new_largest, total, accum)
+        return (running, None)
+
+    stacked = (
+        piece_keys.reshape(count, block, -1),
+        piece_values.reshape(count, block, -1),
+        piece_req.reshape(count, block),
+        piece_pos.reshape(count, block),
+    )
+    state, _ = lax.scan(advance, state, stacked)
+    largest, total, accum = state
+    attn = (
+        (accum / total[..., None])
+        .transpose(2, 0, 1, 3)
+        .reshape(tok_count, query_heads * head_dim)
+        .astype(jnp.bfloat16)
+    )
+    half = tok_count // lax.axis_size("tp")
+    tp_index = lax.axis_index("tp")
+    own_attn = lax.dynamic_slice_in_dim(attn, tp_index * half, half, 0)
+    other_attn = lax.dynamic_slice_in_dim(attn, (1 - tp_index) * half, half, 0)
+    sent = jnp.dot(other_attn, w_out, preferred_element_type=jnp.float32).astype(jnp.bfloat16)
+    proj = jnp.dot(own_attn, w_out, preferred_element_type=jnp.float32)
+    proj = proj + lax.ppermute(sent, "tp", [(0, 1), (1, 0)]).astype(jnp.float32)
+    own_rows = lax.dynamic_slice_in_dim(tokens, lax.axis_index("tp") * half, half, 0)
+    resid = (own_rows.astype(jnp.float32) + proj).astype(jnp.bfloat16)
+    mixed = rms_norm(resid.astype(jnp.float32), post_gain).astype(jnp.bfloat16)
+    top = route_ids.shape[2]
+    weights = route_weights[0]
+    weights = weights / jnp.sum(weights, axis=-1, keepdims=True)
+    high = weights.astype(jnp.bfloat16)
+    low = (weights - high.astype(jnp.float32)).astype(jnp.bfloat16)
+    notes = jnp.concatenate(
+        [
+            route_ids[0].astype(jnp.bfloat16),
+            high,
+            low,
+            jnp.zeros((half, 128 - 3 * top), jnp.bfloat16),
+        ],
+        axis=1,
+    )
+    gathered = gather(jnp.concatenate([mixed, notes], axis=1), True, 2)
+    sources = gathered.reshape(-1, half, width + 128)
+    source_count = sources.shape[0]
+    capacity = 3 * half * top // 64
+    expert = (seq_index * 2 + tp_index) * 2 + lax.axis_index("pd")
+    notes = sources[:, :, width:].astype(jnp.float32)
+    mine = notes[:, :, :top] == expert.astype(jnp.float32)
+    share = jnp.sum(
+        jnp.where(mine, notes[:, :, top : 2 * top] + notes[:, :, 2 * top : 3 * top], 0.0), axis=2
+    )
+    member = jnp.any(mine, axis=2)
+    earlier = (
+        lax.broadcasted_iota(jnp.int32, (half, half), 0)
+        < lax.broadcasted_iota(jnp.int32, (half, half), 1)
+    ).astype(jnp.bfloat16)
+    rank = jnp.dot(
+        member.astype(jnp.bfloat16), earlier, preferred_element_type=jnp.float32
+    ).astype(jnp.int32)
+    seat = jnp.where(member, rank, -1)
+    places = lax.broadcasted_iota(jnp.int32, (source_count, capacity, half), 1)
+    chosen = (seat[:, None, :] == places).astype(jnp.bfloat16)
+    rows = jnp.einsum(
+        "sct,std->scd", chosen, sources[:, :, :width], preferred_element_type=jnp.float32
+    ).astype(jnp.bfloat16)
+    made = expert_mlp(rows[:, None], w_gate_up, w_down)[:, 0]
+    partial = jnp.einsum("sct,scd->std", chosen, made, preferred_element_type=jnp.float32)
+    partial = (partial * share[:, :, None]).astype(jnp.bfloat16)
+    layer_out = combine(partial.reshape(DEPTH, 2, 2, 2, half, width), resid, 3)
+    layer_out = layer_out.astype(jnp.bfloat16)[None]
+    layers = earlier_kv.shape[0]
+    per_device = tok_count // PAGE
+    page_count = layers * per_device
+    seq_size = lax.axis_size("seq")
+    page_cap = max(1, page_count // seq_size)
+    pages = earlier_kv[:, 0].reshape(layers, per_device, PAGE, kv_local, 2 * head_dim)
+    pages = pages.transpose(3, 0, 1, 2, 4).reshape(kv_local, page_count, PAGE, 2 * head_dim)
+    table = page_table[:, 0].transpose(2, 0, 1).reshape(kv_local, page_count)
+    owners = table // page_count
+    slots = table % page_count
+    order = jnp.arange(page_count, dtype=jnp.int32)
+    same = (owners[:, :, None] == owners[:, None, :]) & (
+        order[None, None, :] < order[None, :, None]
+    )
+    page_rank = jnp.sum(same.astype(jnp.int32), axis=2)
+    page_target = owners * page_cap + page_rank
+    head_rows = jnp.broadcast_to(jnp.arange(kv_local, dtype=jnp.int32)[:, None], page_target.shape)
+    outgoing_pages = (
+        jnp.zeros((kv_local, seq_size * page_cap, PAGE, 2 * head_dim), jnp.bfloat16)
+        .at[head_rows, page_target]
+        .set(pages)
+    )
+    outgoing_slots = (
+        jnp.full((kv_local, seq_size * page_cap), -1, jnp.int32)
+        .at[head_rows, page_target]
+        .set(slots)
+    )
+    arrived_pages, arrived_slots = (
+        lax.all_to_all(outgoing_pages, "seq", split_axis=1, concat_axis=1, tiled=True),
+        lax.all_to_all(outgoing_slots, "seq", split_axis=1, concat_axis=1, tiled=True),
+    )
+    placing = (arrived_slots[:, None, :] == order[None, :, None]).astype(jnp.bfloat16)
+    cache = jnp.einsum(
+        "hkr,hrpc->hkpc", placing, arrived_pages, preferred_element_type=jnp.float32
+    ).astype(jnp.bfloat16)
+    decode_cache = cache[None, :, None]
+    return (layer_out, decode_cache)
+
+
 def solution(mesh):
     in_specs = (
         P("pd", "seq", None),
@@ -278,4 +831,6 @@
         P(None, "pd", "seq", "tp"),
     )
     out_specs = (P("pd", ("seq", "tp"), None), P("seq", "tp", "pd", None, None, None))
-    return jax.shard_map(shards, mesh=mesh, in_specs=in_specs, out_specs=out_specs, check_vma=False)
+    small = mesh.shape["seq"] == 2 * DEPTH and mesh.shape["tp"] == 2 and mesh.shape["pd"] == 2
+    per_device = shards_small if small else shards
+    return jax.shard_map(per_device, mesh=mesh, in_specs=in_specs, out_specs=out_specs, check_vma=False)

time: 567 us -> 351 us (0.62)
  waiting for transfers between devices: 276 us -> 1.61 us
  Pallas kernels: 0 us -> 194 us
  blocking collectives: 107 us -> 0 us
  local copies, waits for them, and re-layouts: 58.3 us -> 27.4 us
  other arithmetic: 18.1 us -> 35.9 us
  between operations: 15.5 us -> 1 us
  matrix products: 68.7 us -> 81.7 us
  starting transfers between devices: 17.8 us -> 7.8 us
    all_to_all x4 -> x2, waiting for transfers between devices: 276 us -> 1.61 us  [the longest x1 1.61 us: shards_small(): lax.all_to_all(outgoing_slots, 'seq', split_axis=1, concat_axis=1, tiled=...]
    pallas_call x0 -> x3, Pallas kernels: none -> 194 us  [the longest x2 112 us: gather(): pl.pallas_call(functools.partial(gather_kernel, full), out_shape=jax.Shap...]
    all_gather x2 -> x0, blocking collectives: 70 us -> none  [the longest x1 35.7 us: shards(): piece_keys = lax.all_gather(all_keys, 'seq', axis=0, tiled=True)]
    unnamed x1 -> x0, blocking collectives: 37.1 us -> none
    scatter x3 -> x2, local copies, waits for them, and re-layouts: 28.5 us -> 3.99 us  [the longest x1 3.37 us: shards_small(): outgoing_pages = jnp.zeros((kv_local, seq_size * page_cap, PAGE, 2 * head...]
    dot_general x8 -> x9, matrix products: 25.1 us -> 43.1 us  [the longest x1 15.3 us: shards_small(): jnp.einsum('sct,scd->std', chosen, made, preferred_element_type=jnp.float32)]
    gather x1 -> x0, local copies, waits for them, and re-layouts: 12.4 us -> none  [shards(): gathered = returned.reshape(experts * capacity, width)[target]]
    all_to_all x4 -> x2, starting transfers between devices: 17.8 us -> 7.79 us  [the longest x1 4.47 us: shards_small(): lax.all_to_all(outgoing_pages, 'seq', split_axis=1, concat_axis=1, tiled=...]
  transfers between devices with their start and end apart: 5 -> 3, of which waited for: 3 -> 1; matrix products, arithmetic and copies ran while one was open for 11% -> 17% of each run, Pallas kernels for 0% -> 49%
where the time goes in v1:
time: 351 us; the launch traced here: 350 us
  Pallas kernels  194 us (55%)
  matrix products  81.7 us (23%)
  other arithmetic  35.9 us (10%)
  local copies, waits for them, and re-layouts  27.4 us (8%)
  starting transfers between devices  7.8 us (2%)
    pallas_call x2, Pallas kernels, gather(): pl.pallas_call(functools.partial(gather_kernel, full), out_shape=jax.Shap...  112 us
    pallas_call x1, Pallas kernels, combine(): pl.pallas_call(combine_kernel, out_shape=jax.ShapeDtypeStruct((rows, widt...  81.9 us
    dot_general x1, matrix products, expert_mlp(): jnp.einsum('sejd,edf->sejf', arrived, w_gate_up, preferred_element_type=j...  15.6 us
    dot_general x1, matrix products, shards_small(): jnp.einsum('sct,scd->std', chosen, made, preferred_element_type=jnp.float32)  15.3 us
    dot_general x2, matrix products, advance(): jnp.einsum('hgtd,khd->hgtk', queries, key_heads, preferred_element_type=j...  13.5 us
    reduce_sum x2, other arithmetic, advance(): total = factor * total + jnp.sum(expo, axis=-1)  12.5 us
    dot_general x1, matrix products, shards_small(): jnp.einsum('sct,std->scd', chosen, sources[:, :, :width], preferred_eleme...  10.8 us
    dot_general x2, matrix products, advance(): jnp.einsum('hgtk,khd->hgtd', expo.astype(jnp.bfloat16), value_heads, pref...  9.45 us
  transfers between devices with their start and end apart: 3, of which 1 were waited for; matrix products, arithmetic and copies ran while one was open for 17% of the time, Pallas kernels for 49%

profile of v1, /device:TPU:0, one launch (start us, length us, event | category | flops | bytes accessed | tf_op | source)
XLA Modules:
  0.0 349.8 jit_solution(7783532520029616208)
XLA Ops:
  6.6 1.5 fusion.47
  8.2 1.9 convolution_convert_fusion.2
  10.0 2.0 multiply_reduce_fusion.1
  15.1 1.5 maximum_maximum_fusion.in_ref
  16.6 24.0 %gather_seq.1 = bf16[4,2,320,256]{3,2,1,0:T(8,128)(2,1)} custom-call(bf16[320,256]{1,0:T(8,128)(2,1)} %maximum_maximum_fusion.in_ref), custom_call_target="tpu_custom_call" | custom-call | tf_op jit(solution)/shard_map/gather_seq/pallas_call | solution.py:173
  40.6 2.4 fusion.107
  43.0 6.5 %copy.87 = bf16[1024,2048]{1,0:T(8,128)(2,1)} copy(bf16[1024,2048]{0,1:T(8,128)(2,1)} %bitcast.212) | data formatting | bytes 8388608 | tf_op jit(solution)/shard_map/dot_general | solution.py:633
  49.6 3.9 %multiply_reduce_fusion = (f32[256,8]{0,1:T(8,128)S(1)}, f32[256,8,128]{0,2,1:T(8,128)S(1)}) fusion(bf16[8,128,2048]{2,1,0:T(8,128)(2,1)} %bitcast.213, bf16[1,256,2048]{2,1,0:T(8,128)(2,1)} %param.21, f32[2048]{0:T(1024)S(1)} %copy-done.12, f32[256]{0:T(256)S(1)} %copy-done.10), kind=kOutput, calls=%fused_computation.76 | convolution fusion | flops 1076361216 | bytes 6308864 | tf_op jit(solution)/shard_map/dot_general | solution.py:633
  54.7 2.0 copy.74
  56.7 38.8 %while.15 = (s32[]{:T(128)}, f32[1,8,256]{2,1,0:T(8,128)S(1)}, f32[1,8,256]{2,1,0:T(8,128)S(1)}, f32[1,8,256,128]{3,2,1,0:T(8,128)}, s32[256]{0:T(256)S(1)}, /*i...) while((s32[]{:T(128)}, f32[1,8,256]{2,1,0:T(8,128)S(1)}, ...), condition=%wide.region_16.17_spmd.clone, body=%wide.region_13.16_spmd.clone.sunk | while | flops 1372794880 | bytes 78151864 | solution.py:711
  57.7 6.7 %fusion.123 = (f32[8,256]{1,0:T(8,128)S(1)}, f32[1280,8,256]{2,0,1:T(8,128)}) fusion(pred[256,1280]{0,1:T(8,128)(4,1)S(1)} %compare_and_fusion.2, bf16[1,8,256,128]{3,2,1,0:T(8,128)(2,1)} %get-tuple-element.329, bf16[2,1280,128]{2,1,0:T(8,128)(2,1)} %get-tuple-element.328, s32[]{:T(128)S(6)} %copy.96), kind=kOutput, calls=%fused_computation.6.clone.1 | convolution fusion | flops 678950912 | bytes 11673604 | tf_op jit(solution)/shard_map/while/body/eval_jaxpr/hgtd,khd->hgtk/dot_general | solution.py:688
  64.4 6.3 %fusion.125 = f32[8,256]{1,0:T(8,128)S(1)} fusion(f32[1280,8,256]{2,0,1:T(8,128)} %get-tuple-element.292, f32[8,256]{1,0:T(8,128)S(1)} %bitcast.214, pred[256,1280]{0,1:T(8,128)(4,1)S(1)} %compare_and_fusion.2), kind=kLoop, calls=%fused_computation.5.clone.1 | loop fusion | flops 10483712 | bytes 10829824 | tf_op jit(solution)/shard_map/while/body/eval_jaxpr/reduce_sum | solution.py:695
  71.4 4.6 %fusion.126 = f32[1,8,256,128]{3,2,1,0:T(8,128)} fusion(f32[1280,8,256]{2,0,1:T(8,128)S(1)} %copy-done.3, f32[8,256]{1,0:T(8,128)S(1)} %bitcast.215, pred[256,1280]{0,1:T(8,128)(4,1)S(1)} %compare_and_fusion.2, f32[1,8,256,128]{3,2,1,0:T(8,128)} %get-tuple-element.310, f32[8,256]{1,0:T(8,128)S(1)} %get-tuple-element.293, pred[]{:T(512)S(6)} %compare.41, ...), kind=kOutput, calls=%fused_computation.10.clone.1 | convolution fusion | flops 682360832 | bytes 13254661 | tf_op jit(solution)/shard_map/while/body/eval_jaxpr/hgtk,khd->hgtd/dot_general | solution.py:696
  77.0 6.7 %fusion.123 = (f32[8,256]{1,0:T(8,128)S(1)}, f32[1280,8,256]{2,0,1:T(8,128)}) fusion(pred[256,1280]{0,1:T(8,128)(4,1)S(1)} %compare_and_fusion.2, bf16[1,8,256,128]{3,2,1,0:T(8,128)(2,1)} %get-tuple-element.329, bf16[2,1280,128]{2,1,0:T(8,128)(2,1)} %get-tuple-element.328, s32[]{:T(128)S(6)} %copy.96), kind=kOutput, calls=%fused_computation.6.clone.1 | convolution fusion | flops 678950912 | bytes 11673604 | tf_op jit(solution)/shard_map/while/body/eval_jaxpr/hgtd,khd->hgtk/dot_general | solution.py:688
  83.8 6.3 %fusion.125 = f32[8,256]{1,0:T(8,128)S(1)} fusion(f32[1280,8,256]{2,0,1:T(8,128)} %get-tuple-element.292, f32[8,256]{1,0:T(8,128)S(1)} %bitcast.214, pred[256,1280]{0,1:T(8,128)(4,1)S(1)} %compare_and_fusion.2), kind=kLoop, calls=%fused_computation.5.clone.1 | loop fusion | flops 10483712 | bytes 10829824 | tf_op jit(solution)/shard_map/while/body/eval_jaxpr/reduce_sum | solution.py:695
  90.7 4.8 %fusion.126 = f32[1,8,256,128]{3,2,1,0:T(8,128)} fusion(f32[1280,8,256]{2,0,1:T(8,128)S(1)} %copy-done.3, f32[8,256]{1,0:T(8,128)S(1)} %bitcast.215, pred[256,1280]{0,1:T(8,128)(4,1)S(1)} %compare_and_fusion.2, f32[1,8,256,128]{3,2,1,0:T(8,128)} %get-tuple-element.310, f32[8,256]{1,0:T(8,128)S(1)} %get-tuple-element.293, pred[]{:T(512)S(6)} %compare.41, ...), kind=kOutput, calls=%fused_computation.10.clone.1 | convolution fusion | flops 682360832 | bytes 13254661 | tf_op jit(solution)/shard_map/while/body/eval_jaxpr/hgtk,khd->hgtd/dot_general | solution.py:696
  95.5 2.6 copy.75
  98.1 2.1 divide_convert_fusion
  100.2 3.8 %convolution_convert_fusion = bf16[128,2048]{1,0:T(8,128)(2,1)} fusion(bf16[1024,2048]{1,0:T(8,128)(2,1)} %param.28, bf16[256,1024]{0,1:T(8,128)(2,1)} %bitcast.216, s32[]{:T(128)S(6)} %select_n.96), kind=kOutput, calls=%fused_computation.46 | convolution fusion | flops 537133056 | bytes 4980740 | tf_op jit(solution)/shard_map/dot_general | solution.py:723
  105.9 3.3 all-to-all-start
  110.7 3.4 scatter_fusion
  114.1 1.6 all-to-all-done
  115.7 4.5 %all-to-all-start.1 = ((bf16[1,16,128,256]{3,2,0,1:T(8,128)(2,1)}), bf16[1,16,128,256]{3,2,0,1:T(8,128)(2,1)}, u32[]{:S(2)}, u32[]{:S(2)}) async-start(bf16[1,16,128,256]{3,2,0,1:T(8,128)(2,1)} %bitcast.209), calls=%async_computation.1 | async-start | bytes 2097152 | tf_op jit(solution)/shard_map/all_to_all | solution.py:800
  121.5 3.5 fusion.56
  126.8 1.9 concatenate.59.in_ref
  128.7 88.4 %gather_full.1 = bf16[4,2,2,2,128,2176]{5,4,3,2,1,0:T(8,128)(2,1)} custom-call(bf16[128,2176]{1,0:T(8,128)(2,1)} %concatenate.59.in_ref), custom_call_target="tpu_custom_call" | custom-call | tf_op jit(solution)/shard_map/gather_full/pallas_call | solution.py:173
  219.2 1.7 fusion.53
  221.1 10.8 %fusion.23 = bf16[32,48,2048]{2,1,0:T(8,128)(2,1)} fusion(bf16[32,128,2176]{2,1,0:T(8,128)(2,1)} %bitcast.207, s32[32,128]{1,0:T(8,128)S(1)} %fusion.55), kind=kOutput, calls=%fused_computation.31 | convolution fusion | flops 805502976 | bytes 23085056 | tf_op jit(solution)/shard_map/sct,std->scd/dot_general | solution.py:764
  231.9 15.6 %fusion.29 = f32[32,1,48,1536]{3,2,0,1:T(8,128)} fusion(bf16[1,2048,1536]{2,1,0:T(8,128)(2,1)} %param.36, bf16[32,48,2048]{2,1,0:T(8,128)(2,1)} %fusion.23), kind=kOutput, calls=%fused_computation.37 | convolution fusion | flops 9663676416 | bytes 22020096 | tf_op jit(solution)/shard_map/sejd,edf->sejf/dot_general | solution.py:395
  247.5 15.3 %multiply_convert_fusion = bf16[32,128,2048]{2,1,0:T(8,128)(2,1)} fusion(f32[32,128]{1,0:T(8,128)S(1)} %fusion.53, bf16[1,768,2048]{2,1,0:T(8,128)(2,1)S(1)} %copy-done, f32[32,1,48,1536]{3,2,0,1:T(8,128)} %fusion.29, s32[32,128]{1,0:T(8,128)S(1)} %fusion.55), kind=kOutput, calls=%fused_computation.30 | convolution fusion | flops 5664342016 | bytes 29392896 | tf_op jit(solution)/shard_map/sct,scd->std/dot_general | solution.py:768
  263.8 81.9 %combine.1 = f32[128,2048]{1,0:T(8,128)S(1)} custom-call(bf16[4,2,2,2,128,2048]{5,4,3,2,1,0:T(8,128)(2,1)} %bitcast.208, bf16[128,2048]{1,0:T(8,128)(2,1)S(1)} %copy-done.2), custom_call_target="tpu_custom_call" | custom-call | tf_op jit(solution)/shard_map/combine/pallas_call | solution.py:335
  346.5 1.9 fusion.54
  (107 shorter events, 25.3 us)
Async XLA Ops:
  0.6 246.8 %copy-start = (bf16[1,768,2048]{2,1,0:T(8,128)(2,1)S(1)}, bf16[1,768,2048]{2,1,0:T(8,128)(2,1)}, u32[]{:S(2)}) copy-start(bf16[1,768,2048]{2,1,0:T(8,128)(2,1)} %param.37) | copy-start | bytes 9437188
  0.6 14.5 %copy-start.4 = (bf16[1,64,128]{2,1,0:T(8,128)(2,1)S(1)}, bf16[1,64,128]{2,1,0:T(8,128)(2,1)}, u32[]{:S(2)}) copy-start(bf16[1,64,128]{2,1,0:T(8,128)(2,1)} %param.31) | copy-start | bytes 49156
  8.1 4.0 %copy-start.9 = (f32[256]{0:T(256)}, f32[256]{0:T(256)S(1)}, u32[]{:S(2)}) copy-start(f32[256]{0:T(256)S(1)} %add_rsqrt_fusion.2) | copy-start | bytes 3076
  43.0 6.5 %copy-start.10 = (f32[256]{0:T(256)S(1)}, f32[256]{0:T(256)}, u32[]{:S(2)}) copy-start(f32[256]{0:T(256)} %copy-done.9) | copy-start | bytes 3076
  43.0 6.5 %copy-start.12 = (f32[2048]{0:T(1024)S(1)}, f32[2048]{0:T(1024)}, u32[]{:S(2)}) copy-start(f32[2048]{0:T(1024)} %param.22) | copy-start | bytes 24580
  49.5 3.9 %copy-start.11 = (f32[128]{0:T(128)S(1)}, f32[128]{0:T(128)}, u32[]{:S(2)}) copy-start(f32[128]{0:T(128)} %param.26) | copy-start | bytes 1540
  64.4 7.0 %copy-start.3 = (f32[1280,8,256]{2,0,1:T(8,128)S(1)}, f32[1280,8,256]{2,0,1:T(8,128)}, u32[]{:S(2)}) copy-start(f32[1280,8,256]{2,0,1:T(8,128)} %get-tuple-element.292) | copy-start | bytes 31457284 | tf_op jit(solution)/shard_map/while
  83.7 7.0 %copy-start.3 = (f32[1280,8,256]{2,0,1:T(8,128)S(1)}, f32[1280,8,256]{2,0,1:T(8,128)}, u32[]{:S(2)}) copy-start(f32[1280,8,256]{2,0,1:T(8,128)} %get-tuple-element.292) | copy-start | bytes 31457284 | tf_op jit(solution)/shard_map/while
  95.5 8.5 %copy-start.8 = (s32[8,1,2,1]{0,3,2,1:T(1,128)S(1)}, s32[8,1,2,1]{0,3,2,1:T(1,128)}, u32[]{:S(2)}) copy-start(s32[8,1,2,1]{0,3,2,1:T(1,128)} %param.39) | copy-start | bytes 196
  95.5 13.8 %copy-start.7 = (s32[1,128,8]{1,2,0:T(8,128)S(1)}, s32[1,128,8]{1,2,0:T(8,128)}, u32[]{:S(2)}) copy-start(s32[1,128,8]{1,2,0:T(8,128)} %param.34) | copy-start | bytes 12292
  95.5 13.9 %copy-start.5 = (f32[1,128,8]{1,2,0:T(8,128)S(1)}, f32[1,128,8]{1,2,0:T(8,128)}, u32[]{:S(2)}) copy-start(f32[1,128,8]{1,2,0:T(8,128)} %param.35) | copy-start | bytes 12292
  104.0 17.5 %collective-permute-start = (bf16[128,2048]{1,0:T(8,128)(2,1)}, bf16[128,2048]{1,0:T(8,128)(2,1)}, u32[]{:S(2)}, u32[]{:S(2)}) collective-permute-start(bf16[128,2048]{1,0:T(8,128)(2,1)} %convolution_convert_fusion), channel_id=1, source_target_pairs={{0,2},{2,0},{1,3},{3,1},{4,6},{6,4},{5,7},{7,5},{8,10},{10,8},{9,1... | collective-permute-start | bytes 1572872 | tf_op jit(solution)/shard_map/ppermute | solution.py:725
  105.9 9.7 %all-to-all-start = ((s32[1,8,2]{2,0,1:T(1,128)}), s32[1,8,2]{2,0,1:T(1,128)S(1)}, u32[]{:S(2)}, u32[]{:S(2)}) async-start(s32[1,8,2]{2,0,1:T(1,128)} %bitcast.49), calls=%async_computation | async-start | bytes 8192 | tf_op jit(solution)/shard_map/all_to_all | solution.py:801
  114.1 10.9 %copy-start.6 = (f32[2048]{0:T(1024)S(1)}, f32[2048]{0:T(1024)}, u32[]{:S(2)}) copy-start(f32[2048]{0:T(1024)} %param.29) | copy-start | bytes 24580
  115.7 230.9 %all-to-all-start.1 = ((bf16[1,16,128,256]{3,2,0,1:T(8,128)(2,1)}), bf16[1,16,128,256]{3,2,0,1:T(8,128)(2,1)}, u32[]{:S(2)}, u32[]{:S(2)}) async-start(bf16[1,16,128,256]{3,2,0,1:T(8,128)(2,1)} %bitcast.209), calls=%async_computation.1 | async-start | bytes 2097152 | tf_op jit(solution)/shard_map/all_to_all | solution.py:800
  126.0 0.8 copy-start.1
  262.7 1.0 copy-start.2

commit v2 on v1

--- a/solution.py
+++ b/solution.py
@@ -372,8 +372,13 @@
     )
 
 
+def running_sum(counts):
+    index = jnp.arange(counts.shape[0], dtype=jnp.int32)
+    return jnp.sum(jnp.where(index[None, :] <= index[:, None], counts[None, :], 0), axis=1)
+
+
 def query_places(lengths, context_lengths, places):
-    ends = jnp.cumsum(lengths)
+    ends = running_sum(lengths)
     starts = ends - lengths
     request = jnp.sum((places[:, None] >= ends[None, :]).astype(jnp.int32), axis=1)
     member = request[:, None] == jnp.arange(lengths.shape[0], dtype=jnp.int32)[None, :]
@@ -383,7 +388,7 @@
 
 
 def context_places(context_lengths, places):
-    ends = jnp.cumsum(context_lengths)
+    ends = running_sum(context_lengths)
     starts = ends - context_lengths
     request = jnp.sum((places[:, None] >= ends[None, :]).astype(jnp.int32), axis=1)
     member = request[:, None] == jnp.arange(context_lengths.shape[0], dtype=jnp.int32)[None, :]
@@ -640,6 +645,40 @@
         rms_norm(query.reshape(tok_count, query_heads, head_dim), q_gain), query_pos
     ).astype(jnp.bfloat16)
     queries = queries.reshape(tok_count, kv_local, group, head_dim).transpose(1, 2, 0, 3)
+    layers = earlier_kv.shape[0]
+    per_device = tok_count // PAGE
+    page_count = layers * per_device
+    seq_size = lax.axis_size("seq")
+    page_cap = max(1, page_count // seq_size)
+    pages = earlier_kv[:, 0].reshape(layers, per_device, PAGE, kv_local, 2 * head_dim)
+    pages = pages.transpose(3, 0, 1, 2, 4).reshape(kv_local, page_count, PAGE, 2 * head_dim)
+    table = page_table[:, 0].transpose(2, 0, 1).reshape(kv_local, page_count)
+    owners = table // page_count
+    slots = table % page_count
+    order = jnp.arange(page_count, dtype=jnp.int32)
+    same = (owners[:, :, None] == owners[:, None, :]) & (
+        order[None, None, :] < order[None, :, None]
+    )
+    page_rank = jnp.sum(same.astype(jnp.int32), axis=2)
+    page_target = owners * page_cap + page_rank
+    head_rows = jnp.broadcast_to(jnp.arange(kv_local, dtype=jnp.int32)[:, None], page_target.shape)
+    outgoing_pages = (
+        jnp.zeros((kv_local, seq_size * page_cap, PAGE, 2 * head_dim), jnp.bfloat16)
+        .at[head_rows, page_target]
+        .set(pages)
+    )
+    outgoing_slots = (
+        jnp.full((kv_local, seq_size * page_cap), -1, jnp.int32)
+        .at[head_rows, page_target]
+        .set(slots)
+    )
+    queries, outgoing_pages, outgoing_slots = lax.optimization_barrier(
+        (queries, outgoing_pages, outgoing_slots)
+    )
+    arrived_pages, arrived_slots = (
+        lax.all_to_all(outgoing_pages, "seq", split_axis=1, concat_axis=1, tiled=True),
+        lax.all_to_all(outgoing_slots, "seq", split_axis=1, concat_axis=1, tiled=True),
+    )
     span_keys = rotate(
         rms_norm(key_proj.reshape(tok_count, kv_local, head_dim), k_gain), query_pos
     ).astype(jnp.bfloat16)
@@ -723,6 +762,9 @@
     sent = jnp.dot(other_attn, w_out, preferred_element_type=jnp.float32).astype(jnp.bfloat16)
     proj = jnp.dot(own_attn, w_out, preferred_element_type=jnp.float32)
     proj = proj + lax.ppermute(sent, "tp", [(0, 1), (1, 0)]).astype(jnp.float32)
+    proj, arrived_pages, arrived_slots = lax.optimization_barrier(
+        (proj, arrived_pages, arrived_slots)
+    )
     own_rows = lax.dynamic_slice_in_dim(tokens, lax.axis_index("tp") * half, half, 0)
     resid = (own_rows.astype(jnp.float32) + proj).astype(jnp.bfloat16)
     mixed = rms_norm(resid.astype(jnp.float32), post_gain).astype(jnp.bfloat16)
@@ -769,37 +811,6 @@
     partial = (partial * share[:, :, None]).astype(jnp.bfloat16)
     layer_out = combine(partial.reshape(DEPTH, 2, 2, 2, half, width), resid, 3)
     layer_out = layer_out.astype(jnp.bfloat16)[None]
-    layers = earlier_kv.shape[0]
-    per_device = tok_count // PAGE
-    page_count = layers * per_device
-    seq_size = lax.axis_size("seq")
-    page_cap = max(1, page_count // seq_size)
-    pages = earlier_kv[:, 0].reshape(layers, per_device, PAGE, kv_local, 2 * head_dim)
-    pages = pages.transpose(3, 0, 1, 2, 4).reshape(kv_local, page_count, PAGE, 2 * head_dim)
-    table = page_table[:, 0].transpose(2, 0, 1).reshape(kv_local, page_count)
-    owners = table // page_count
-    slots = table % page_count
-    order = jnp.arange(page_count, dtype=jnp.int32)
-    same = (owners[:, :, None] == owners[:, None, :]) & (
-        order[None, None, :] < order[None, :, None]
-    )
-    page_rank = jnp.sum(same.astype(jnp.int32), axis=2)
-    page_target = owners * page_cap + page_rank
-    head_rows = jnp.broadcast_to(jnp.arange(kv_local, dtype=jnp.int32)[:, None], page_target.shape)
-    outgoing_pages = (
-        jnp.zeros((kv_local, seq_size * page_cap, PAGE, 2 * head_dim), jnp.bfloat16)
-        .at[head_rows, page_target]
-        .set(pages)
-    )
-    outgoing_slots = (
-        jnp.full((kv_local, seq_size * page_cap), -1, jnp.int32)
-        .at[head_rows, page_target]
-        .set(slots)
-    )
-    arrived_pages, arrived_slots = (
-        lax.all_to_all(outgoing_pages, "seq", split_axis=1, concat_axis=1, tiled=True),
-        lax.all_to_all(outgoing_slots, "seq", split_axis=1, concat_axis=1, tiled=True),
-    )
     placing = (arrived_slots[:, None, :] == order[None, :, None]).astype(jnp.bfloat16)
     cache = jnp.einsum(
         "hkr,hrpc->hkpc", placing, arrived_pages, preferred_element_type=jnp.float32

time: 351 us -> 321 us (0.915)
  Pallas kernels: 194 us -> 179 us
  matrix products: 81.7 us -> 71.9 us
  other arithmetic: 35.9 us -> 26.7 us
  starting transfers between devices: 7.8 us -> 11.7 us
    pallas_call x2, Pallas kernels: 112 us -> 103 us  [gather(): pl.pallas_call(functools.partial(gather_kernel, full), out_shape=jax.Shap...]
    reduce_sum x2, other arithmetic: 12.5 us -> 4.25 us  [advance(): total = factor * total + jnp.sum(expo, axis=-1)]
    dot_general x2, matrix products: 13.5 us -> 5.55 us  [advance(): jnp.einsum('hgtd,khd->hgtk', queries, key_heads, preferred_element_type=j...]
    pallas_call x1, Pallas kernels: 81.9 us -> 76.3 us  [combine(): pl.pallas_call(combine_kernel, out_shape=jax.ShapeDtypeStruct((rows, widt...]
    all_to_all x1, starting transfers between devices: 3.33 us -> 7.29 us  [shards_small(): lax.all_to_all(outgoing_slots, 'seq', split_axis=1, concat_axis=1, tiled=...]
  transfers between devices with their start and end apart: 3 -> 3, of which waited for: 1 -> 1; matrix products, arithmetic and copies ran while one was open for 17% -> 14% of each run, Pallas kernels for 49% -> 7%
where the time goes in v2:
time: 321 us; the launch traced here: 320 us
  Pallas kernels  179 us (56%)
  matrix products  71.9 us (22%)
  local copies, waits for them, and re-layouts  28.8 us (9%)
  other arithmetic  26.7 us (8%)
  starting transfers between devices  11.7 us (4%)
    pallas_call x2, Pallas kernels, gather(): pl.pallas_call(functools.partial(gather_kernel, full), out_shape=jax.Shap...  103 us
    pallas_call x1, Pallas kernels, combine(): pl.pallas_call(combine_kernel, out_shape=jax.ShapeDtypeStruct((rows, widt...  76.3 us
    dot_general x1, matrix products, expert_mlp(): jnp.einsum('sejd,edf->sejf', arrived, w_gate_up, preferred_element_type=j...  15.6 us
    dot_general x1, matrix products, shards_small(): jnp.einsum('sct,scd->std', chosen, made, preferred_element_type=jnp.float32)  15.3 us
    dot_general x1, matrix products, shards_small(): jnp.einsum('sct,std->scd', chosen, sources[:, :, :width], preferred_eleme...  10.8 us
    all_to_all x1, starting transfers between devices, shards_small(): lax.all_to_all(outgoing_slots, 'seq', split_axis=1, concat_axis=1, tiled=...  7.29 us
    dot_general x1, local copies, waits for them, and re-layouts, shards_small(): query = jnp.dot(normed, w_query, preferred_element_type=jnp.float32)  6.5 us
  transfers between devices with their start and end apart: 3, of which 1 were waited for; matrix products, arithmetic and copies ran while one was open for 14% of the time, Pallas kernels for 7%

profile of v2, /device:TPU:0, one launch (start us, length us, event | category | flops | bytes accessed | tf_op | source)
XLA Modules:
  0.0 320.1 jit_solution(15802148408390804743)
XLA Ops:
  3.3 1.5 fusion.47
  5.1 6.5 %copy.88 = bf16[1024,2048]{1,0:T(8,128)(2,1)} copy(bf16[1024,2048]{0,1:T(8,128)(2,1)} %bitcast.211) | data formatting | bytes 8388608 | tf_op jit(solution)/shard_map/dot_general | solution.py:638
  11.7 4.9 %multiply_reduce_fusion = (f32[256,8]{0,1:T(8,128)S(1)}, f32[256,8,128]{0,2,1:T(8,128)}) fusion(bf16[8,128,2048]{2,1,0:T(8,128)(2,1)} %bitcast.212, bf16[1,256,2048]{2,1,0:T(8,128)(2,1)} %param.21, f32[2048]{0:T(1024)S(1)} %copy-done.17, f32[256]{0:T(256)S(1)} %add_rsqrt_fusion.2), kind=kOutput, calls=%fused_computation.76 | convolution fusion | flops 1076361216 | bytes 6308864 | tf_op jit(solution)/shard_map/dot_general | solution.py:638
  18.7 3.4 %scatter_fusion = bf16[16,128,256]{2,1,0:T(8,128)(2,1)} fusion(bf16[16,128,256]{2,1,0:T(8,128)(2,1)} %broadcast.484, s32[16]{0:T(128)S(1)} %fusion.96, bf16[16,128,256]{2,1,0:T(8,128)(2,1)} %bitcast.217), kind=kCustom, calls=%fused_computation | custom fusion | bytes 3145792 | tf_op jit(solution)/shard_map/scatter | solution.py:668
  22.1 1.4 multiply_multiply_fusion
  26.3 7.3 %all-to-all-start.1 = ((s32[1,8,2]{2,0,1:T(1,128)}), s32[1,8,2]{2,0,1:T(1,128)}, u32[]{:S(2)}, u32[]{:S(2)}) async-start(s32[1,8,2]{2,0,1:T(1,128)} %bitcast.35), calls=%async_computation.1 | async-start | bytes 8192 | tf_op jit(solution)/shard_map/all_to_all | solution.py:680
  34.6 1.9 convolution_convert_fusion.2
  36.5 2.0 multiply_reduce_fusion.1
  42.0 22.4 %gather_seq.1 = bf16[4,2,320,256]{3,2,1,0:T(8,128)(2,1)} custom-call(bf16[320,256]{1,0:T(8,128)(2,1)} %maximum_maximum_fusion.in_ref), custom_call_target="tpu_custom_call" | custom-call | tf_op jit(solution)/shard_map/gather_seq/pallas_call | solution.py:173
  64.4 2.4 fusion.107
  66.9 2.1 copy.78
  68.9 4.4 %all-to-all-start = ((bf16[1,16,128,256]{3,2,0,1:T(8,128)(2,1)}), bf16[1,16,128,256]{3,2,0,1:T(8,128)(2,1)}, u32[]{:S(2)}, u32[]{:S(2)}) async-start(bf16[1,16,128,256]{3,2,0,1:T(8,128)(2,1)} %bitcast.208), calls=%async_computation | async-start | bytes 2097152 | tf_op jit(solution)/shard_map/all_to_all | solution.py:679
  73.3 19.8 %while.15 = (s32[]{:T(128)}, f32[1,8,256]{2,1,0:T(8,128)S(1)}, f32[1,8,256]{2,1,0:T(8,128)S(1)}, f32[1,8,256,128]{3,2,1,0:T(8,128)}, s32[256]{0:T(256)S(1)}, /*i...) while((s32[]{:T(128)}, f32[1,8,256]{2,1,0:T(8,128)S(1)}, ...), condition=%wide.region_19.20_spmd.clone, body=%wide.region_16.19_spmd.clone.sunk | while | flops 1372794880 | bytes 47218928 | solution.py:750
  74.3 2.8 fusion.123
  77.1 2.1 fusion.125
  79.3 3.0 fusion.126
  84.2 2.8 fusion.123
  87.0 2.1 fusion.125
  89.2 3.0 fusion.126
  93.2 2.6 copy.79
  97.9 3.7 %convolution_convert_fusion = bf16[128,2048]{1,0:T(8,128)(2,1)} fusion(bf16[1024,2048]{1,0:T(8,128)(2,1)} %param.28, bf16[256,1024]{0,1:T(8,128)(2,1)S(1)} %bitcast.215, s32[]{:T(128)S(6)} %select_n.110), kind=kOutput, calls=%fused_computation.46 | convolution fusion | flops 537133056 | bytes 4980740 | tf_op jit(solution)/shard_map/dot_general | solution.py:762
  103.8 4.1 %convert_add_fusion.1 = f32[128,2048]{1,0:T(8,128)} fusion(bf16[128,2048]{1,0:T(8,128)(2,1)} %collective-permute-done, bf16[1024,2048]{1,0:T(8,128)(2,1)} %param.28, bf16[256,1024]{0,1:T(8,128)(2,1)} %bitcast.216, s32[]{:T(128)S(6)} %select_n.98), kind=kOutput, calls=%fused_computation.73 | convolution fusion | flops 537395200 | bytes 6029316 | tf_op jit(solution)/shard_map/dot_general | solution.py:763
  107.9 1.6 fusion.56
  109.5 2.1 fusion.54
  114.0 1.9 concatenate.60.in_ref
  115.8 80.4 %gather_full.1 = bf16[4,2,2,2,128,2176]{5,4,3,2,1,0:T(8,128)(2,1)} custom-call(bf16[128,2176]{1,0:T(8,128)(2,1)} %concatenate.60.in_ref), custom_call_target="tpu_custom_call" | custom-call | tf_op jit(solution)/shard_map/gather_full/pallas_call | solution.py:173
  196.3 1.5 slice_convert_fusion
  198.4 1.7 fusion.53
  200.2 10.8 %fusion.23 = bf16[32,48,2048]{2,1,0:T(8,128)(2,1)} fusion(bf16[32,128,2176]{2,1,0:T(8,128)(2,1)} %bitcast.206, s32[32,128]{1,0:T(8,128)S(1)} %fusion.55), kind=kOutput, calls=%fused_computation.31 | convolution fusion | flops 805502976 | bytes 23085056 | tf_op jit(solution)/shard_map/sct,std->scd/dot_general | solution.py:806
  211.0 15.6 %fusion.29 = f32[32,1,48,1536]{3,2,0,1:T(8,128)} fusion(bf16[1,2048,1536]{2,1,0:T(8,128)(2,1)} %param.36, bf16[32,48,2048]{2,1,0:T(8,128)(2,1)} %fusion.23), kind=kOutput, calls=%fused_computation.37 | convolution fusion | flops 9663676416 | bytes 22020096 | tf_op jit(solution)/shard_map/sejd,edf->sejf/dot_general | solution.py:400
  226.6 15.3 %multiply_convert_fusion = bf16[32,128,2048]{2,1,0:T(8,128)(2,1)} fusion(f32[32,128]{1,0:T(8,128)S(1)} %fusion.53, bf16[1,768,2048]{2,1,0:T(8,128)(2,1)S(1)} %copy-done, f32[32,1,48,1536]{3,2,0,1:T(8,128)} %fusion.29, s32[32,128]{1,0:T(8,128)S(1)} %fusion.55), kind=kOutput, calls=%fused_computation.30 | convolution fusion | flops 5664342016 | bytes 29392896 | tf_op jit(solution)/shard_map/sct,scd->std/dot_general | solution.py:810
  242.9 76.3 %combine.1 = f32[128,2048]{1,0:T(8,128)S(1)} custom-call(bf16[4,2,2,2,128,2048]{5,4,3,2,1,0:T(8,128)(2,1)} %bitcast.207, bf16[128,2048]{1,0:T(8,128)(2,1)S(1)} %copy-done.2), custom_call_target="tpu_custom_call" | custom-call | tf_op jit(solution)/shard_map/combine/pallas_call | solution.py:335
  (123 shorter events, 25.4 us)
Async XLA Ops:
  0.6 226.0 %copy-start = (bf16[1,768,2048]{2,1,0:T(8,128)(2,1)S(1)}, bf16[1,768,2048]{2,1,0:T(8,128)(2,1)}, u32[]{:S(2)}) copy-start(bf16[1,768,2048]{2,1,0:T(8,128)(2,1)} %param.37) | copy-start | bytes 9437188
  0.7 16.0 %copy-start.13 = (f32[64]{0:T(128)}, f32[64]{0:T(128)S(1)}, u32[]{:S(2)}) copy-start(f32[64]{0:T(128)S(1)} %multiply_exponential_fusion) | copy-start | bytes 772
  3.3 8.4 %copy-start.17 = (f32[2048]{0:T(1024)S(1)}, f32[2048]{0:T(1024)}, u32[]{:S(2)}) copy-start(f32[2048]{0:T(1024)} %param.22) | copy-start | bytes 24580
  4.8 29.8 %copy-start.15 = (f32[256]{0:T(256)}, f32[256]{0:T(256)S(1)}, u32[]{:S(2)}) copy-start(f32[256]{0:T(256)S(1)} %add_rsqrt_fusion.2) | copy-start | bytes 3076
  11.6 4.9 %copy-start.14 = (s32[1,8]{1,0:T(1,128)S(1)}, s32[1,8]{1,0:T(1,128)}, u32[]{:S(2)}) copy-start(s32[1,8]{1,0:T(1,128)} %param.33) | copy-start | bytes 100
  11.7 10.5 %copy-start.16 = (f32[128]{0:T(128)S(1)}, f32[128]{0:T(128)}, u32[]{:S(2)}) copy-start(f32[128]{0:T(128)} %param.26) | copy-start | bytes 1540
  16.6 17.3 %copy-start.10 = (f32[256]{0:T(256)}, f32[256]{0:T(256)S(1)}, u32[]{:S(2)}) copy-start(f32[256]{0:T(256)S(1)} %get-tuple-element.207) | copy-start | bytes 3076
  23.5 17.7 %copy-start.7 = (bf16[1,64,128]{2,1,0:T(8,128)(2,1)S(1)}, bf16[1,64,128]{2,1,0:T(8,128)(2,1)}, u32[]{:S(2)}) copy-start(bf16[1,64,128]{2,1,0:T(8,128)(2,1)} %param.31) | copy-start | bytes 49156
  23.5 17.7 %copy-start.8 = (bf16[1,64,128]{2,1,0:T(8,128)(2,1)S(1)}, bf16[1,64,128]{2,1,0:T(8,128)(2,1)}, u32[]{:S(2)}) copy-start(bf16[1,64,128]{2,1,0:T(8,128)(2,1)} %param.30) | copy-start | bytes 49156
  26.3 42.6 %all-to-all-start.1 = ((s32[1,8,2]{2,0,1:T(1,128)}), s32[1,8,2]{2,0,1:T(1,128)}, u32[]{:S(2)}, u32[]{:S(2)}) async-start(s32[1,8,2]{2,0,1:T(1,128)} %bitcast.35), calls=%async_computation.1 | async-start | bytes 8192 | tf_op jit(solution)/shard_map/all_to_all | solution.py:680
  68.9 39.0 %all-to-all-start = ((bf16[1,16,128,256]{3,2,0,1:T(8,128)(2,1)}), bf16[1,16,128,256]{3,2,0,1:T(8,128)(2,1)}, u32[]{:S(2)}, u32[]{:S(2)}) async-start(bf16[1,16,128,256]{3,2,0,1:T(8,128)(2,1)} %bitcast.208), calls=%async_computation | async-start | bytes 2097152 | tf_op jit(solution)/shard_map/all_to_all | solution.py:679
  77.1 2.2 copy-start.4
  77.1 2.2 copy-start.6
  82.3 1.0 copy-start.5
  87.0 2.2 copy-start.4
  87.0 2.2 copy-start.6
  92.2 1.0 copy-start.5
  93.2 8.4 %copy-start.9 = (f32[1,128,8]{1,2,0:T(8,128)S(1)}, f32[1,128,8]{1,2,0:T(8,128)}, u32[]{:S(2)}) copy-start(f32[1,128,8]{1,2,0:T(8,128)} %param.35) | copy-start | bytes 12292
  93.2 8.5 %copy-start.12 = (s32[1,128,8]{1,2,0:T(8,128)S(1)}, s32[1,128,8]{1,2,0:T(8,128)}, u32[]{:S(2)}) copy-start(s32[1,128,8]{1,2,0:T(8,128)} %param.34) | copy-start | bytes 12292
  97.0 0.8 copy-start.3
  101.6 2.3 collective-permute-start
  103.3 9.7 %copy-start.11 = (f32[2048]{0:T(1024)S(1)}, f32[2048]{0:T(1024)}, u32[]{:S(2)}) copy-start(f32[2048]{0:T(1024)} %param.29) | copy-start | bytes 24580
  109.5 3.5 %copy-start.1 = (bf16[128,2048]{1,0:T(8,128)(2,1)}, bf16[128,2048]{1,0:T(8,128)(2,1)S(1)}, u32[]{:S(2)}) copy-start(bf16[128,2048]{1,0:T(8,128)(2,1)S(1)} %get-tuple-element.206.resid_ref) | copy-start | bytes 1572868
  241.9 1.0 copy-start.2
